TPU v7x, 256 devices: a whole 4x4x8 slice. The times are simulated.
256 devices in a mesh: seq: 64 (over z, x, core), chan: 4 (over y).
Axes of the slice: x: 4, y: 4, z: 8, core: 2. Of those that a mesh axis runs over, the one named last changes fastest.
Arguments:
- qkv: bfloat16 [32768, 3, 8192], P(('seq', 'chan')), may hold values from -6 to 6
- short_filter: float32 [3, 7, 512], replicated, may hold values from -2 to 2
- rates: float32 [16, 8192], P(None, 'chan'), as said below
- residue: float32 [16, 8192], P(None, 'chan'), may hold values from -1.5 to 1.5
Outputs:
- mixed: bfloat16 [32768, 8192], P('seq', 'chan')
Inputs may be any that keep to these rules, and one draw needn't show every extreme that they name: `rates`: every decay rate is positive, at least 0.1 / 32768 and at most 1 / 30.
All inputs are finite; a program needn't handle non-finite values.
Results may differ from a plain program's by a relative error of at most 0.011.
Values may be sent and summed in bfloat16 or wider, within the bound.
No kernel may reach another device: no remote copies, remote signals or barrier semaphores. Data moves between devices by JAX's collectives and lax.ppermute only.
A program may use at most 320 MiB of HBM per device.

v0:
```python
import functools

import jax
import jax.numpy as jnp
from jax import lax
from jax.experimental import pallas as pl
from jax.experimental.pallas import tpu as pltpu
from jax.sharding import PartitionSpec as P

TAPS = 7
GROUP = 16
MODES = 16
CHUNK = 1024
SUB = 8
LANES = 128
LEAD = 8
HEAD = 16
XS = 4
CORES = 2
VMEM_LIMIT = 60 * 1024 * 1024
COST = pl.CostEstimate(flops=1, bytes_accessed=1, transcendentals=0)
BF16 = jnp.bfloat16
F32 = jnp.float32


def featurize_stream(taps_ref, scr, stream, start, step):
    taps = [taps_ref[0, pl.ds((stream * TAPS + lag) * SUB, SUB), :] for lag in range(TAPS)]
    window = [
        scr[stream, pl.ds(pl.multiple_of((start + LEAD - (TAPS - 1) + n) * SUB, SUB), SUB), :]
        for n in range(step + TAPS - 1)
    ]
    summed = []
    for token in range(step):
        total = taps[0] * window[token + TAPS - 1]
        for lag in range(1, TAPS):
            total = total + taps[lag] * window[token + TAPS - 1 - lag]
        summed.append(total)
    return [jnp.concatenate([summed[n], summed[n + 1]], 0).astype(BF16) for n in range(0, step, 2)]


def featurize_tokens(taps_ref, scr, start, step):
    query, k, v = [featurize_stream(taps_ref, scr, stream, start, step) for stream in range(3)]
    return query, [(a.astype(F32) * b.astype(F32)).astype(BF16) for a, b in zip(k, v)]


def featurize_kernel(chunks_ref, raw_ref, taps_ref, *rest):
    out_refs, scr = rest[:-1], rest[-1]
    count = len(out_refs) // 2
    rows = raw_ref.shape[1]
    for stream in range(3):
        scr[stream, pl.ds(0, LEAD * SUB), :] = jnp.zeros((LEAD * SUB, LANES), F32)
        for tile in range(SUB):
            cols = pl.ds(tile * LANES, LANES)
            for part in range(rows // 16):
                value = raw_ref[stream, pl.ds(part * 16, 16), cols].astype(F32)
                scr[stream, pl.ds((LEAD + part * 16) * SUB + tile, 16, stride=SUB), :] = value

    step = 8
    for n in range(count):

        @pl.when(pl.program_id(0) // 2 == n)
        def _(query_ref=out_refs[n], gated_ref=out_refs[count + n]):
            def body(index, carry):
                start = index * step
                query, gated = featurize_tokens(taps_ref, scr, start, step)
                for k in range(step // 2):
                    at = pl.ds(pl.multiple_of((start + 2 * k) * SUB, 2 * SUB), 2 * SUB)
                    query_ref[0, at, :] = query[k]
                    gated_ref[0, at, :] = gated[k]
                return carry

            lax.fori_loop(0, rows // step, body, 0)


def featurize(chunks, raw, taps, count):
    rows = raw.shape[1]

    def turn(n):
        return pl.BlockSpec((1, rows * SUB, LANES), lambda i, b: (jnp.clip(i - 2 * n, 0, 1), 0, 0))

    return pl.pallas_call(
        featurize_kernel,
        out_shape=(jax.ShapeDtypeStruct((2, rows * SUB, LANES), BF16),) * (2 * count),
        grid_spec=pltpu.PrefetchScalarGridSpec(
            num_scalar_prefetch=1,
            grid=(2 * count,),
            in_specs=[
                pl.BlockSpec((3, rows, CHUNK), lambda i, b: (0, 0, b[i])),
                pl.BlockSpec((1, 3 * TAPS * SUB, LANES), lambda i, b: (b[i], 0, 0)),
            ],
            out_specs=[turn(n) for n in range(count)] * 2,
            scratch_shapes=[pltpu.VMEM((3, (LEAD + rows) * SUB, LANES), F32)],
        ),
        compiler_params=pltpu.CompilerParams(vmem_limit_bytes=VMEM_LIMIT),
        cost_estimate=COST,
        name="featurize",
    )(chunks, raw, taps)


def head_kernel(chunks_ref, raw_ref, halo_ref, taps_ref, *rest):
    scr = rest[-1]
    out_refs = rest[len(rest) // 2 : -1]
    count = len(out_refs) // 2
    for n in range(count):
        chunk = chunks_ref[2 * n + pl.program_id(0)]
        for stream in range(3):
            for tile in range(SUB):
                cols = pl.ds(pl.multiple_of(chunk * CHUNK + tile * LANES, LANES), LANES)
                scr[stream, pl.ds(tile, LEAD, stride=SUB), :] = halo_ref[stream, :, cols].astype(F32)
                value = raw_ref[stream, :, cols].astype(F32)
                scr[stream, pl.ds(LEAD * SUB + tile, HEAD, stride=SUB), :] = value
        for start in range(0, HEAD, 8):
            query, gated = featurize_tokens(taps_ref.at[pl.ds(chunk, 1)], scr, start, 8)
            for k in range(4):
                at = pl.ds((start + 2 * k) * SUB, 2 * SUB)
                out_refs[n][0, at, :] = query[k]
                out_refs[count + n][0, at, :] = gated[k]


def featurize_head(chunks, raw, halo, taps, featured):
    count = len(featured)
    return pl.pallas_call(
        head_kernel,
        out_shape=tuple(jax.ShapeDtypeStruct(v.shape, v.dtype) for v in featured),
        grid_spec=pltpu.PrefetchScalarGridSpec(
            num_scalar_prefetch=1,
            grid=(2,),
            in_specs=[
                pl.BlockSpec((3, HEAD, raw.shape[2]), lambda i, b: (0, 0, 0)),
                pl.BlockSpec(halo.shape, lambda i, b: (0, 0, 0)),
                pl.BlockSpec(taps.shape, lambda i, b: (0, 0, 0)),
            ]
            + [pl.BlockSpec(memory_space=pl.ANY)] * count,
            out_specs=[pl.BlockSpec((1, HEAD * SUB, LANES), lambda i, b: (i, 0, 0))] * count,
            scratch_shapes=[pltpu.VMEM((3, (LEAD + HEAD) * SUB, LANES), F32)],
        ),
        input_output_aliases={4 + n: n for n in range(count)},
        compiler_params=pltpu.CompilerParams(vmem_limit_bytes=VMEM_LIMIT),
        cost_estimate=COST,
        name="featurize_head",
    )(chunks, raw, halo, taps, *featured)


def tree_sum(values):
    while len(values) > 1:
        values = [a + b for a, b in zip(values[::2], values[1::2])]
    return values[0]


def ends_kernel(*refs, count):
    gated_refs, decay_ref, ends_ref = refs[:count], refs[count], refs[count + 1]
    tokens = gated_refs[0].shape[1] // SUB
    decay = [decay_ref[0, pl.ds(m * SUB, SUB), :] for m in range(MODES)]
    step = 8

    def run(gated_ref):
        def body(index, states):
            for n in range(0, step, 2):
                at = pl.multiple_of((index * step + n) * SUB, 2 * SUB)
                pair = gated_ref[0, pl.ds(at, 2 * SUB), :].astype(F32)
                for half in range(2):
                    entry = pair[half * SUB : (half + 1) * SUB]
                    states = [d * s + entry for d, s in zip(decay, states)]
            return tuple(states)

        zero = jnp.zeros((SUB, LANES), F32)
        states = lax.fori_loop(0, tokens // step, body, (zero,) * MODES)
        for m in range(MODES):
            ends_ref[0, pl.ds(m * SUB, SUB), :] = states[m]

    if count == 1:
        run(gated_refs[0])
        return
    for n in range(count):

        @pl.when(pl.program_id(0) // 2 == n)
        def _(gated_ref=gated_refs[n]):
            run(gated_ref)


def ends_part(gated, decay):
    count = len(gated)
    rows = gated[0].shape[1]

    def turn(n):
        return pl.BlockSpec((1, rows, LANES), lambda i: (jnp.clip(i - 2 * n, 0, 1), 0, 0))

    state = (1, MODES * SUB, LANES)
    return pl.pallas_call(
        functools.partial(ends_kernel, count=count),
        out_shape=jax.ShapeDtypeStruct((2 * count, MODES * SUB, LANES), F32),
        grid=(2 * count,),
        in_specs=[turn(n) for n in range(count)] + [pl.BlockSpec(state, lambda i: (i % 2, 0, 0))],
        out_specs=pl.BlockSpec(state, lambda i: (i, 0, 0)),
        compiler_params=pltpu.CompilerParams(vmem_limit_bytes=VMEM_LIMIT),
        cost_estimate=COST,
        name="block_ends",
    )(*gated, decay)


def in_turn(n, rows):
    return pl.BlockSpec((1, rows, LANES), lambda e, t, p: (jnp.where((e == 0) & (t <= p[n]), 0, 1), 0, 0))


def response_kernel(place_ref, starts_ref, decay_ref, gain_ref, *rest):
    out_ref, state_ref, scr = rest[-3:]
    count = (len(rest) - 3) // 2
    tokens = rest[0].shape[1] // SUB
    decay = [decay_ref[0, pl.ds(m * SUB, SUB), :] for m in range(MODES)]
    gain = [gain_ref[0, pl.ds(m * SUB, SUB), :] for m in range(MODES)]
    step = 4
    turn = pl.program_id(1)

    @pl.when(turn == 0)
    def _():
        state_ref[...] = starts_ref[0]

    for n in range(count):

        @pl.when(place_ref[n] == turn)
        def _(gated_ref=rest[n], query_ref=rest[count + n]):
            def body(index, states):
                for k in range(0, step, 2):
                    at = pl.multiple_of((index * step + k) * SUB, 2 * SUB)
                    pair = gated_ref[0, pl.ds(at, 2 * SUB), :].astype(F32)
                    queries = query_ref[0, pl.ds(at, 2 * SUB), :].astype(F32)
                    for half in range(2):
                        part = slice(half * SUB, (half + 1) * SUB)
                        states = [d * s + pair[part] for d, s in zip(decay, states)]
                        response = tree_sum([g * s for g, s in zip(gain, states)])
                        scr[pl.ds(at + half * SUB, SUB), :] = queries[part] * response
                return tuple(states)

            states = tuple(state_ref[pl.ds(m * SUB, SUB), :] for m in range(MODES))
            states = lax.fori_loop(0, tokens // step, body, states)
            for m in range(MODES):
                state_ref[pl.ds(m * SUB, SUB), :] = states[m]

    for tile in range(SUB):
        for part in range(tokens // 16):
            value = scr[pl.ds(part * 16 * SUB + tile, 16, stride=SUB), :]
            out_ref[pl.ds(part * 16, 16), pl.ds(tile * LANES, LANES)] = value.astype(BF16)


def response_part(places, starts, decay, gain, gated, queries):
    count = len(gated)
    rows = gated[0].shape[1]
    tokens = rows // SUB
    state = pl.BlockSpec((1, MODES * SUB, LANES), lambda e, t, p: (e, 0, 0))
    return pl.pallas_call(
        response_kernel,
        out_shape=jax.ShapeDtypeStruct((count * tokens, 2 * CHUNK), BF16),
        grid_spec=pltpu.PrefetchScalarGridSpec(
            num_scalar_prefetch=1,
            grid=(2, count),
            in_specs=[state] * 3 + [in_turn(n, rows) for n in range(count)] * 2,
            out_specs=pl.BlockSpec((tokens, CHUNK), lambda e, t, p: (t, e)),
            scratch_shapes=[
                pltpu.VMEM((MODES * SUB, LANES), F32),
                pltpu.VMEM((rows, LANES), F32),
            ],
        ),
        compiler_params=pltpu.CompilerParams(vmem_limit_bytes=VMEM_LIMIT),
        cost_estimate=COST,
        name="response",
    )(places, starts, decay, gain, *gated, *queries)


def local(qkv, short_filter, rates, residue):
    seqs, chans = lax.axis_size("seq"), lax.axis_size("chan")
    zs = seqs // (XS * CORES)
    seq = lax.axis_index("seq")
    c = lax.axis_index("chan")
    h = seq % CORES
    x = (seq // CORES) % XS
    rows = qkv.shape[0]

    def permute(value, move):
        pairs = []
        for z0 in range(zs):
            for x0 in range(XS):
                for h0 in range(CORES):
                    to = move(z0, x0, h0)
                    if to is not None:
                        z1, x1, h1 = to
                        pairs.append(((z0 * XS + x0) * CORES + h0, (z1 * XS + x1) * CORES + h1))
        return lax.ppermute(value, "seq", pairs)

    def shift_y(value, by):
        return lax.ppermute(value, "chan", [(n, (n + by) % chans) for n in range(chans)])

    def shift_x(value, by):
        return permute(value, lambda z0, x0, h0: (z0, (x0 + by) % XS, h0))

    def shift_z(value, by):
        return permute(value, lambda z0, x0, h0: (z0 + by, x0, h0) if z0 + by < zs else None)

    def swap_core(value):
        return permute(value, lambda z0, x0, h0: (z0, x0, 1 - h0))

    raw = jnp.transpose(qkv, (1, 0, 2))
    following = [(n, n + 1) for n in range(seqs * chans - 1)]
    halo = lax.ppermute(raw[:, -LEAD:, :], ("seq", "chan"), following)

    small = jnp.transpose(short_filter.reshape(3 * TAPS, -1, SUB, LANES // GROUP), (1, 0, 2, 3))
    spread = jnp.repeat(jnp.eye(LANES // GROUP, dtype=F32), GROUP, axis=1)
    taps = jnp.dot(
        small.reshape(-1, LANES // GROUP), spread, precision=lax.Precision.HIGHEST
    ).reshape(-1, 3 * TAPS * SUB, LANES)

    def chunked(value):
        pieces = jnp.transpose(value.reshape(MODES, 2, SUB, LANES), (1, 0, 2, 3))
        return pieces.reshape(2, MODES * SUB, LANES)

    rate = chunked(rates)
    gain = chunked(residue * jnp.sqrt(-jnp.expm1(-2.0 * rates)))
    decay = jnp.exp(-rate)

    order = (2, 1, 3, 0)
    away = order[:3]
    chunks = jnp.stack([2 * ((c + dy) % chans) + e for dy in order for e in range(2)]).astype(jnp.int32)
    places = jnp.stack([(c - dy) % chans for dy in order]).astype(jnp.int32)
    featured = featurize(chunks, raw, taps, chans)
    featured, halo = lax.optimization_barrier((featured, halo))
    featured = featurize_head(chunks, raw, halo, taps, featured)
    query, gated = featured[:chans], featured[chans:]
    gated_in = [shift_y(gated[n], dy) for n, dy in enumerate(away)] + [gated[3]]
    query_in = [shift_y(query[n], dy) for n, dy in enumerate(away)] + [query[3]]

    powers = [jnp.exp(-rate * float(rows * n)) for n in range(chans)]

    def power(n):
        value = powers[0]
        for k in range(1, chans):
            value = jnp.where(n == k, powers[k], value)
        return value

    weights = lax.optimization_barrier(tuple(power(chans - 1 - places[n]) for n in range(chans)))
    ends_own = ends_part([gated_in[3]], decay)
    ends_first = ends_part([gated_in[0]], decay)
    ends_first, gated_in[1], gated_in[2] = lax.optimization_barrier((ends_first, gated_in[1], gated_in[2]))
    ends_rest = ends_part(gated_in[1:3], decay)
    total = weights[0] * ends_first + weights[1] * ends_rest[:2] + weights[2] * ends_rest[2:] + weights[3] * ends_own

    block = float(rows * chans)
    span = 2.0 * block
    wide = span * XS
    mine = lax.dynamic_index_in_dim(total, h, 0, keepdims=False)
    other = lax.dynamic_index_in_dim(total, 1 - h, 0, keepdims=False)
    rate_h = lax.dynamic_index_in_dim(rate, h, 0, keepdims=False)
    partner = swap_core(other)
    first = jnp.where(h == 0, mine, partner)
    second = jnp.where(h == 0, partner, mine)
    decay_block = jnp.exp(-rate_h * block)
    pair = decay_block * first + second

    pair, query_in[0] = lax.optimization_barrier((pair, query_in[0]))
    from_x = {s: shift_x(pair, s) for s in range(1, XS)}
    before_x = sum(
        jnp.where(s <= x, jnp.exp(-rate_h * (span * (s - 1))) * from_x[s], 0.0) for s in range(1, XS)
    )
    plane = jnp.exp(-rate_h * (span * (XS - 1 - x).astype(F32))) * pair
    for s in range(1, XS):
        steps = (XS - 1 - (x - s) % XS).astype(F32)
        plane = plane + jnp.exp(-rate_h * (span * steps)) * from_x[s]

    near = {s: shift_z(plane, s) for s in range(1, 4)}
    before_z = near[1] + jnp.exp(-rate_h * wide) * near[2] + jnp.exp(-rate_h * (2 * wide)) * near[3]
    window = plane + jnp.exp(-rate_h * wide) * before_z
    window, query_in[1], query_in[2] = lax.optimization_barrier((window, query_in[1], query_in[2]))
    for far in range(4, zs, 4):
        before_z = before_z + jnp.exp(-rate_h * (wide * (far - 1))) * shift_z(window, far)
    entering = jnp.exp(-rate_h * (span * x.astype(F32))) * before_z + before_x
    later = decay_block * entering + first
    own_start = jnp.where(h == 0, entering, later)
    other_start = swap_core(jnp.where(h == 0, later, entering))
    starts = jnp.stack(
        [jnp.where(h == 0, own_start, other_start), jnp.where(h == 0, other_start, own_start)]
    )
    return response_part(places, starts, decay, gain, gated_in, query_in)


def solution(mesh):
    placed = (P(("seq", "chan"), None, None), P(), P(None, "chan"), P(None, "chan"))
    return jax.shard_map(
        local, mesh=mesh, in_specs=placed, out_specs=P("seq", "chan"), check_vma=False
    )
```

profile of v0, /device:TPU:1, one launch (start us, length us, event | category | flops | bytes accessed | tf_op | source)
XLA Modules:
  0.0 120.2 jit_solution(6550540248615905245)
XLA Ops:
  1.0 4.0 %collective-permute-start = (bf16[3,8,8192]{2,1,0:T(8,128)(2,1)S(1)}, bf16[3,8,8192]{2,1,0:T(8,128)(2,1)S(1)}, u32[]{:S(2)}, u32[]{:S(2)}) collective-permute-start(bf16[3,8,8192]{2,1,0:T(8,128)(2,1)S(1)} %slice.12), channel_id=1, source_target_pairs={{0,1},{1,2},{2,3},{3,4},{4,5},{5,6},{6,7},{7,8},{8,9},{9,10},{10,1... | collective-permute-start | bytes 1179656 | tf_op jit(solution)/shard_map/ppermute | solution.py:303
  5.1 1.2 reshape.64
  8.1 2.1 %fusion.23 = f32[128,1344]{0,1:T(8,128)} fusion(f32[8,128]{1,0:T(8,128)S(1)} %reshape.63, f32[1344,8]{0,1:T(8,128)S(1)} %reshape.65), kind=kOutput, calls=%fused_computation.60 | convolution fusion | flops 16515072 | bytes 735232 | tf_op jit(solution)/shard_map/dot_general | solution.py:307
  10.2 14.3 %featurize.1 = (bf16[2,1024,128]{2,1,0:T(8,128)(2,1)}, bf16[2,1024,128]{2,1,0:T(8,128)(2,1)}, bf16[2,1024,128]{2,1,0:T(8,128)(2,1)}, bf16[2,1024,128]{2,1,0:T(8,...) custom-call(s32[8]{0:T(128)} %stack.64.chunks_ref, ...), custom_call_target="tpu_custom_call" | custom-call | flops 1 | bytes 1 | tf_op jit(solution)/shard_map/featurize/pallas_call | solution.py:81
  25.3 4.1 %featurize_head.1 = (bf16[2,1024,128]{2,1,0:T(8,128)(2,1)}, bf16[2,1024,128]{2,1,0:T(8,128)(2,1)}, bf16[2,1024,128]{2,1,0:T(8,128)(2,1)}, bf16[2,1024,128]{2,1,0...) custom-call(s32[8]{0:T(128)} %stack.64.chunks_ref, ...), custom_call_target="tpu_custom_call", output_to_operand_aliasing={{0}: (4, {}), {1}: (5, {}), {2}: (6, {}), {3}: (7, {}), {4}... | custom-call | flops 1 | bytes 1 | tf_op jit(solution)/shard_map/featurize_head/pallas_call | solution.py:122
  29.4 2.7 %collective-permute-start.1 = (bf16[2,1024,128]{2,1,0:T(8,128)(2,1)}, bf16[2,1024,128]{2,1,0:T(8,128)(2,1)S(1)}, u32[]{:S(2)}, u32[]{:S(2)}) collective-permute-start(bf16[2,1024,128]{2,1,0:T(8,128)(2,1)} %get-tuple-element.60), channel_id=1, source_target_pairs={{0,2},{1,3},{2,0},{3,1},{4,6},{5,7},{6,4},{7,5},{8,10},{9,11},{10,... | collective-permute-start | bytes 1572872 | tf_op jit(solution)/shard_map/ppermute | solution.py:290
  32.9 1.8 %collective-permute-start.3 = (bf16[2,1024,128]{2,1,0:T(8,128)(2,1)}, bf16[2,1024,128]{2,1,0:T(8,128)(2,1)S(1)}, u32[]{:S(2)}, u32[]{:S(2)}) collective-permute-start(bf16[2,1024,128]{2,1,0:T(8,128)(2,1)} %get-tuple-element.62), channel_id=1, source_target_pairs={{0,3},{1,0},{2,1},{3,2},{4,7},{5,4},{6,5},{7,6},{8,11},{9,8},{10,9... | collective-permute-start | bytes 1572872 | tf_op jit(solution)/shard_map/ppermute | solution.py:290
  35.6 2.9 %block_ends.5 = f32[2,128,128]{2,1,0:T(8,128)} custom-call(bf16[2,1024,128]{2,1,0:T(8,128)(2,1)} %get-tuple-element.69.refs_0_.rest_3_, f32[2,128,128]{2,1,0:T(8,128)} %get-tuple-element.86.refs_1_.refs_2_.decay_ref), custom_call_target="tpu_custom_call" | custom-call | flops 1 | bytes 1 | tf_op jit(solution)/shard_map/block_ends/pallas_call | solution.py:189
  38.4 5.2 %collective-permute-done.1.refs_0_.rest_0_ = bf16[2,1024,128]{2,1,0:T(8,128)(2,1)S(1)} collective-permute-done((bf16[2,1024,128]{2,1,0:T(8,128)(2,1)}, bf16[2,1024,128]{2,1,0:T(8,128)(2,1)S(1)}, u32[]{:S(2)}, u32[]{:S(2)}) %collective-permute-start.1) | collective-permute-done | bytes 524320 | tf_op jit(solution)/shard_map/ppermute | solution.py:290
  44.5 2.9 %block_ends.3 = f32[2,128,128]{2,1,0:T(8,128)} custom-call(bf16[2,1024,128]{2,1,0:T(8,128)(2,1)} %copy-done, f32[2,128,128]{2,1,0:T(8,128)} %get-tuple-element.86.refs_1_.refs_2_.decay_ref), custom_call_target="tpu_custom_call" | custom-call | flops 1 | bytes 1 | tf_op jit(solution)/shard_map/block_ends/pallas_call | solution.py:189
  47.3 10.2 %collective-permute-done.2.refs_0_.rest_1_ = bf16[2,1024,128]{2,1,0:T(8,128)(2,1)S(1)} collective-permute-done((bf16[2,1024,128]{2,1,0:T(8,128)(2,1)}, bf16[2,1024,128]{2,1,0:T(8,128)(2,1)S(1)}, u32[]{:S(2)}, u32[]{:S(2)}) %collective-permute-start.2) | collective-permute-done | bytes 524320 | tf_op jit(solution)/shard_map/ppermute | solution.py:290
  59.2 4.6 %block_ends.4 = f32[4,128,128]{2,1,0:T(8,128)} custom-call(bf16[2,1024,128]{2,1,0:T(8,128)(2,1)} %copy-done.1, bf16[2,1024,128]{2,1,0:T(8,128)(2,1)} %copy-done.2, f32[2,128,128]{2,1,0:T(8,128)} %get-tuple-element.86.refs_1_.refs_2_.decay_ref), custom_call_target="tpu_custom_call" | custom-call | flops 1 | bytes 1 | tf_op jit(solution)/shard_map/block_ends/pallas_call | solution.py:189
  66.6 1.3 %collective-permute-start.6 = (f32[128,128]{1,0:T(8,128)S(1)}, f32[128,128]{1,0:T(8,128)S(1)}, u32[]{:S(2)}, u32[]{:S(2)}) collective-permute-start(f32[128,128]{1,0:T(8,128)S(1)} %fusion.17), channel_id=1, source_target_pairs={{0,8},{4,12},{8,16},{12,20},{16,24},{20,28},{24,0},{28,4},{32,40},... | collective-permute-start | bytes 196616 | tf_op jit(solution)/shard_map/ppermute | solution.py:287
  67.9 2.5 %collective-permute-start.7 = (f32[128,128]{1,0:T(8,128)S(1)}, f32[128,128]{1,0:T(8,128)S(1)}, u32[]{:S(2)}, u32[]{:S(2)}) collective-permute-start(f32[128,128]{1,0:T(8,128)S(1)} %fusion.17), channel_id=1, source_target_pairs={{0,16},{4,20},{8,24},{12,28},{16,0},{20,4},{24,8},{28,12},{32,48},... | collective-permute-start | bytes 196616 | tf_op jit(solution)/shard_map/ppermute | solution.py:287
  70.3 1.2 collective-permute-start.8
  71.5 1.2 collective-permute-start.12
  72.6 2.4 %collective-permute-start.13 = (bf16[2,1024,128]{2,1,0:T(8,128)(2,1)}, bf16[2,1024,128]{2,1,0:T(8,128)(2,1)S(1)}, u32[]{:S(2)}, u32[]{:S(2)}) collective-permute-start(bf16[2,1024,128]{2,1,0:T(8,128)(2,1)} %get-tuple-element.73), channel_id=1, source_target_pairs={{0,3},{1,0},{2,1},{3,2},{4,7},{5,4},{6,5},{7,6},{8,11},{9,8},{10,9... | collective-permute-start | bytes 1572872 | tf_op jit(solution)/shard_map/ppermute | solution.py:290
  75.1 4.9 %collective-permute-start.10 = (f32[128,128]{1,0:T(8,128)S(1)}, f32[128,128]{1,0:T(8,128)S(1)}, u32[]{:S(2)}, u32[]{:S(2)}) collective-permute-start(f32[128,128]{1,0:T(8,128)S(1)} %fusion.14), channel_id=1, source_target_pairs={{0,64},{4,68},{8,72},{12,76},{16,80},{20,84},{24,88},{28,92},{32,9... | collective-permute-start | bytes 196616 | tf_op jit(solution)/shard_map/ppermute | solution.py:287
  80.0 6.6 %collective-permute-start.11 = (f32[128,128]{1,0:T(8,128)S(1)}, f32[128,128]{1,0:T(8,128)S(1)}, u32[]{:S(2)}, u32[]{:S(2)}) collective-permute-start(f32[128,128]{1,0:T(8,128)S(1)} %fusion.14), channel_id=1, source_target_pairs={{0,96},{4,100},{8,104},{12,108},{16,112},{20,116},{24,120},{28,124... | collective-permute-start | bytes 196616 | tf_op jit(solution)/shard_map/ppermute | solution.py:287
  86.6 2.6 %collective-permute-start.9 = (f32[128,128]{1,0:T(8,128)S(1)}, f32[128,128]{1,0:T(8,128)S(1)}, u32[]{:S(2)}, u32[]{:S(2)}) collective-permute-start(f32[128,128]{1,0:T(8,128)S(1)} %fusion.14), channel_id=1, source_target_pairs={{0,32},{4,36},{8,40},{12,44},{16,48},{20,52},{24,56},{28,60},{32,6... | collective-permute-start | bytes 196616 | tf_op jit(solution)/shard_map/ppermute | solution.py:287
  89.2 1.9 %collective-permute-done.9 = f32[128,128]{1,0:T(8,128)S(1)} collective-permute-done((f32[128,128]{1,0:T(8,128)S(1)}, f32[128,128]{1,0:T(8,128)S(1)}, u32[]{:S(2)}, u32[]{:S(2)}) %collective-permute-start.9) | collective-permute-done | bytes 65568 | tf_op jit(solution)/shard_map/ppermute | solution.py:287
  91.2 6.2 %collective-permute-start.14 = (f32[128,128]{1,0:T(8,128)S(1)}, f32[128,128]{1,0:T(8,128)S(1)}, u32[]{:S(2)}, u32[]{:S(2)}) collective-permute-start(f32[128,128]{1,0:T(8,128)S(1)} %get-tuple-element.74), channel_id=1, source_target_pairs={{0,128},{4,132},{8,136},{12,140},{16,144},{20,148},{24,152},{28,15... | collective-permute-start | bytes 196616 | tf_op jit(solution)/shard_map/ppermute | solution.py:287
  98.8 3.4 %collective-permute-start.15 = (f32[128,128]{1,0:T(8,128)S(1)}, f32[128,128]{1,0:T(8,128)S(1)}, u32[]{:S(2)}, u32[]{:S(2)}) collective-permute-start(f32[128,128]{1,0:T(8,128)S(1)} %get-tuple-element.79), channel_id=1, source_target_pairs={{0,4},{4,0},{8,12},{12,8},{16,20},{20,16},{24,28},{28,24},{32,36},... | collective-permute-start | bytes 196616 | tf_op jit(solution)/shard_map/ppermute | solution.py:287
  103.8 16.4 %response.1 = bf16[512,2048]{1,0:T(8,128)(2,1)} custom-call(s32[4]{0:T(128)} %pad_add_fusion.place_ref, f32[2,128,128]{2,1,0:T(8,128)} %pad_maximum_fusion.starts_ref, f32[2,128,128]{2,1,0:T(8,128)} %get-tuple-element.86.refs_1_.refs_2_.decay_ref, f32[2,128,128]{2,1,0:T(8,128)} %bitcast.157, bf16[2,1024,128]{2,1,0:T(8,128)(2,1)} %copy-done, ...), custom_call_target="tpu_custom_call" | custom-call | flops 1 | bytes 1 | tf_op jit(solution)/shard_map/response/pallas_call | solution.py:250
  (56 shorter events, 13.5 us)
Async XLA Ops:
  1.0 23.5 %collective-permute-start = (bf16[3,8,8192]{2,1,0:T(8,128)(2,1)S(1)}, bf16[3,8,8192]{2,1,0:T(8,128)(2,1)S(1)}, u32[]{:S(2)}, u32[]{:S(2)}) collective-permute-start(bf16[3,8,8192]{2,1,0:T(8,128)(2,1)S(1)} %slice.12), channel_id=1, source_target_pairs={{0,1},{1,2},{2,3},{3,4},{4,5},{5,6},{6,7},{7,8},{8,9},{9,10},{10,1... | collective-permute-start | bytes 1179656 | tf_op jit(solution)/shard_map/ppermute | solution.py:303
  24.5 10.3 %copy-start.3 = (f32[16,2048]{1,0:T(8,128)S(1)}, f32[16,2048]{1,0:T(8,128)}, u32[]{:S(2)}) copy-start(f32[16,2048]{1,0:T(8,128)} %param.6) | copy-start | bytes 393220
  29.3 68.0 %copy-start.8 = (f32[16,2048]{1,0:T(8,128)S(1)}, f32[16,2048]{1,0:T(8,128)}, u32[]{:S(2)}) copy-start(f32[16,2048]{1,0:T(8,128)} %param.7) | copy-start | bytes 393220
  29.4 14.3 %collective-permute-start.1 = (bf16[2,1024,128]{2,1,0:T(8,128)(2,1)}, bf16[2,1024,128]{2,1,0:T(8,128)(2,1)S(1)}, u32[]{:S(2)}, u32[]{:S(2)}) collective-permute-start(bf16[2,1024,128]{2,1,0:T(8,128)(2,1)} %get-tuple-element.60), channel_id=1, source_target_pairs={{0,2},{1,3},{2,0},{3,1},{4,6},{5,7},{6,4},{7,5},{8,10},{9,11},{10,... | collective-permute-start | bytes 1572872 | tf_op jit(solution)/shard_map/ppermute | solution.py:290
  32.1 25.5 %collective-permute-start.2 = (bf16[2,1024,128]{2,1,0:T(8,128)(2,1)}, bf16[2,1024,128]{2,1,0:T(8,128)(2,1)S(1)}, u32[]{:S(2)}, u32[]{:S(2)}) collective-permute-start(bf16[2,1024,128]{2,1,0:T(8,128)(2,1)} %get-tuple-element.61), channel_id=1, source_target_pairs={{0,1},{1,2},{2,3},{3,0},{4,5},{5,6},{6,7},{7,4},{8,9},{9,10},{10,1... | collective-permute-start | bytes 1572872 | tf_op jit(solution)/shard_map/ppermute | solution.py:290
  32.9 24.7 %collective-permute-start.3 = (bf16[2,1024,128]{2,1,0:T(8,128)(2,1)}, bf16[2,1024,128]{2,1,0:T(8,128)(2,1)S(1)}, u32[]{:S(2)}, u32[]{:S(2)}) collective-permute-start(bf16[2,1024,128]{2,1,0:T(8,128)(2,1)} %get-tuple-element.62), channel_id=1, source_target_pairs={{0,3},{1,0},{2,1},{3,2},{4,7},{5,4},{6,5},{7,6},{8,11},{9,8},{10,9... | collective-permute-start | bytes 1572872 | tf_op jit(solution)/shard_map/ppermute | solution.py:290
  35.6 31.0 %collective-permute-start.5 = (bf16[2,1024,128]{2,1,0:T(8,128)(2,1)}, bf16[2,1024,128]{2,1,0:T(8,128)(2,1)S(1)}, u32[]{:S(2)}, u32[]{:S(2)}) collective-permute-start(bf16[2,1024,128]{2,1,0:T(8,128)(2,1)} %get-tuple-element.70), channel_id=1, source_target_pairs={{0,2},{1,3},{2,0},{3,1},{4,6},{5,7},{6,4},{7,5},{8,10},{9,11},{10,... | collective-permute-start | bytes 1572872 | tf_op jit(solution)/shard_map/ppermute | solution.py:290
  43.6 0.8 copy-start
  57.6 0.8 copy-start.1
  58.4 0.8 copy-start.2
  65.0 1.6 %collective-permute-start.4 = (f32[128,128]{1,0:T(8,128)S(1)}, f32[128,128]{1,0:T(8,128)S(1)}, u32[]{:S(2)}, u32[]{:S(2)}) collective-permute-start(f32[128,128]{1,0:T(8,128)S(1)} %dynamic-slice_bitcast_fusion), channel_id=1, source_target_pairs={{0,4},{4,0},{8,12},{12,8},{16,20},{20,16},{24,28},{28,24},{32,36},... | collective-permute-start | bytes 196616 | tf_op jit(solution)/shard_map/ppermute | solution.py:287
  66.6 37.2 %copy-start.4 = (bf16[2,1024,128]{2,1,0:T(8,128)(2,1)}, bf16[2,1024,128]{2,1,0:T(8,128)(2,1)S(1)}, u32[]{:S(2)}) copy-start(bf16[2,1024,128]{2,1,0:T(8,128)(2,1)S(1)} %collective-permute-done.5.rest_4_) | copy-start | bytes 1572868
  66.6 8.4 %collective-permute-start.6 = (f32[128,128]{1,0:T(8,128)S(1)}, f32[128,128]{1,0:T(8,128)S(1)}, u32[]{:S(2)}, u32[]{:S(2)}) collective-permute-start(f32[128,128]{1,0:T(8,128)S(1)} %fusion.17), channel_id=1, source_target_pairs={{0,8},{4,12},{8,16},{12,20},{16,24},{20,28},{24,0},{28,4},{32,40},... | collective-permute-start | bytes 196616 | tf_op jit(solution)/shard_map/ppermute | solution.py:287
  67.9 7.1 %collective-permute-start.7 = (f32[128,128]{1,0:T(8,128)S(1)}, f32[128,128]{1,0:T(8,128)S(1)}, u32[]{:S(2)}, u32[]{:S(2)}) collective-permute-start(f32[128,128]{1,0:T(8,128)S(1)} %fusion.17), channel_id=1, source_target_pairs={{0,16},{4,20},{8,24},{12,28},{16,0},{20,4},{24,8},{28,12},{32,48},... | collective-permute-start | bytes 196616 | tf_op jit(solution)/shard_map/ppermute | solution.py:287
  70.3 4.7 %collective-permute-start.8 = (f32[128,128]{1,0:T(8,128)S(1)}, f32[128,128]{1,0:T(8,128)S(1)}, u32[]{:S(2)}, u32[]{:S(2)}) collective-permute-start(f32[128,128]{1,0:T(8,128)S(1)} %fusion.17), channel_id=1, source_target_pairs={{0,24},{4,28},{8,0},{12,4},{16,8},{20,12},{24,16},{28,20},{32,56},... | collective-permute-start | bytes 196616 | tf_op jit(solution)/shard_map/ppermute | solution.py:287
  71.5 19.7 %collective-permute-start.12 = (bf16[2,1024,128]{2,1,0:T(8,128)(2,1)}, bf16[2,1024,128]{2,1,0:T(8,128)(2,1)S(1)}, u32[]{:S(2)}, u32[]{:S(2)}) collective-permute-start(bf16[2,1024,128]{2,1,0:T(8,128)(2,1)} %get-tuple-element.72), channel_id=1, source_target_pairs={{0,1},{1,2},{2,3},{3,0},{4,5},{5,6},{6,7},{7,4},{8,9},{9,10},{10,1... | collective-permute-start | bytes 1572872 | tf_op jit(solution)/shard_map/ppermute | solution.py:290
  72.6 18.5 %collective-permute-start.13 = (bf16[2,1024,128]{2,1,0:T(8,128)(2,1)}, bf16[2,1024,128]{2,1,0:T(8,128)(2,1)S(1)}, u32[]{:S(2)}, u32[]{:S(2)}) collective-permute-start(bf16[2,1024,128]{2,1,0:T(8,128)(2,1)} %get-tuple-element.73), channel_id=1, source_target_pairs={{0,3},{1,0},{2,1},{3,2},{4,7},{5,4},{6,5},{7,6},{8,11},{9,8},{10,9... | collective-permute-start | bytes 1572872 | tf_op jit(solution)/shard_map/ppermute | solution.py:290
  75.1 14.1 %collective-permute-start.10 = (f32[128,128]{1,0:T(8,128)S(1)}, f32[128,128]{1,0:T(8,128)S(1)}, u32[]{:S(2)}, u32[]{:S(2)}) collective-permute-start(f32[128,128]{1,0:T(8,128)S(1)} %fusion.14), channel_id=1, source_target_pairs={{0,64},{4,68},{8,72},{12,76},{16,80},{20,84},{24,88},{28,92},{32,9... | collective-permute-start | bytes 196616 | tf_op jit(solution)/shard_map/ppermute | solution.py:287
  80.0 9.2 %collective-permute-start.11 = (f32[128,128]{1,0:T(8,128)S(1)}, f32[128,128]{1,0:T(8,128)S(1)}, u32[]{:S(2)}, u32[]{:S(2)}) collective-permute-start(f32[128,128]{1,0:T(8,128)S(1)} %fusion.14), channel_id=1, source_target_pairs={{0,96},{4,100},{8,104},{12,108},{16,112},{20,116},{24,120},{28,124... | collective-permute-start | bytes 196616 | tf_op jit(solution)/shard_map/ppermute | solution.py:287
  86.6 4.5 %collective-permute-start.9 = (f32[128,128]{1,0:T(8,128)S(1)}, f32[128,128]{1,0:T(8,128)S(1)}, u32[]{:S(2)}, u32[]{:S(2)}) collective-permute-start(f32[128,128]{1,0:T(8,128)S(1)} %fusion.14), channel_id=1, source_target_pairs={{0,32},{4,36},{8,40},{12,44},{16,48},{20,52},{24,56},{28,60},{32,6... | collective-permute-start | bytes 196616 | tf_op jit(solution)/shard_map/ppermute | solution.py:287
  91.2 12.6 %copy-start.5 = (bf16[2,1024,128]{2,1,0:T(8,128)(2,1)}, bf16[2,1024,128]{2,1,0:T(8,128)(2,1)S(1)}, u32[]{:S(2)}) copy-start(bf16[2,1024,128]{2,1,0:T(8,128)(2,1)S(1)} %collective-permute-done.12.rest_5_) | copy-start | bytes 1572868
  91.2 12.6 %copy-start.6 = (bf16[2,1024,128]{2,1,0:T(8,128)(2,1)}, bf16[2,1024,128]{2,1,0:T(8,128)(2,1)S(1)}, u32[]{:S(2)}) copy-start(bf16[2,1024,128]{2,1,0:T(8,128)(2,1)S(1)} %collective-permute-done.13.rest_6_) | copy-start | bytes 1572868
  91.2 7.5 %collective-permute-start.14 = (f32[128,128]{1,0:T(8,128)S(1)}, f32[128,128]{1,0:T(8,128)S(1)}, u32[]{:S(2)}, u32[]{:S(2)}) collective-permute-start(f32[128,128]{1,0:T(8,128)S(1)} %get-tuple-element.74), channel_id=1, source_target_pairs={{0,128},{4,132},{8,136},{12,140},{16,144},{20,148},{24,152},{28,15... | collective-permute-start | bytes 196616 | tf_op jit(solution)/shard_map/ppermute | solution.py:287
  98.8 4.3 %collective-permute-start.15 = (f32[128,128]{1,0:T(8,128)S(1)}, f32[128,128]{1,0:T(8,128)S(1)}, u32[]{:S(2)}, u32[]{:S(2)}) collective-permute-start(f32[128,128]{1,0:T(8,128)S(1)} %get-tuple-element.79), channel_id=1, source_target_pairs={{0,4},{4,0},{8,12},{12,8},{16,20},{20,16},{24,28},{28,24},{32,36},... | collective-permute-start | bytes 196616 | tf_op jit(solution)/shard_map/ppermute | solution.py:287
  (1 other events, 0.8 us)
where the time goes:
time: 121 us; the launch traced here: 120 us
  Pallas kernels  45.1 us (37%)
  starting transfers between devices  42.2 us (35%)
  waiting for transfers between devices  19 us (16%)
  local copies, waits for them, and re-layouts  7.92 us (7%)
  other arithmetic  3.57 us (3%)
  matrix products  2.11 us (2%)
    ppermute x9, starting transfers between devices, permute(): return lax.ppermute(value, 'seq', pairs)  29.2 us
    pallas_call x1, Pallas kernels, response_part(): pl.pallas_call(response_kernel, out_shape=jax.ShapeDtypeStruct((count * t...  16.4 us
    ppermute x6, waiting for transfers between devices, shift_y(): lax.ppermute(value, 'chan', [(n, (n + by) % chans) for n in range(chans)])  15.4 us
    pallas_call x1, Pallas kernels, featurize(): pl.pallas_call(featurize_kernel, out_shape=(jax.ShapeDtypeStruct((2, rows...  14.3 us
    pallas_call x3, Pallas kernels, ends_part(): pl.pallas_call(functools.partial(ends_kernel, count=count), out_shape=jax...  10.3 us
    ppermute x6, starting transfers between devices, shift_y(): lax.ppermute(value, 'chan', [(n, (n + by) % chans) for n in range(chans)])  8.91 us
    pallas_call x1, Pallas kernels, featurize_head(): pl.pallas_call(head_kernel, out_shape=tuple((jax.ShapeDtypeStruct(v.shape...  4.08 us
    ppermute x1, starting transfers between devices, local(): halo = lax.ppermute(raw[:, -LEAD:, :], ('seq', 'chan'), following)  4.03 us
  transfers between devices with their start and end apart: 16, of which 6 were waited for; matrix products, arithmetic and copies ran while one was open for 7% of the time, Pallas kernels for 20%

commit v1 on v0

--- a/solution.py
+++ b/solution.py
@@ -55,7 +55,7 @@
                 value = raw_ref[stream, pl.ds(part * 16, 16), cols].astype(F32)
                 scr[stream, pl.ds((LEAD + part * 16) * SUB + tile, 16, stride=SUB), :] = value
 
-    step = 8
+    step = 16
     for n in range(count):
 
         @pl.when(pl.program_id(0) // 2 == n)
@@ -208,7 +208,7 @@
     tokens = rest[0].shape[1] // SUB
     decay = [decay_ref[0, pl.ds(m * SUB, SUB), :] for m in range(MODES)]
     gain = [gain_ref[0, pl.ds(m * SUB, SUB), :] for m in range(MODES)]
-    step = 4
+    step = 8
     turn = pl.program_id(1)
 
     @pl.when(turn == 0)

time: 121 us -> 119 us (0.983)
  Pallas kernels: 45.1 us -> 43.5 us
where the time goes in v1:
time: 119 us
  Pallas kernels  43.5 us (37%)
  starting transfers between devices  42.2 us (35%)
  waiting for transfers between devices  19 us (16%)
  local copies, waits for them, and re-layouts  7.92 us (7%)
  other arithmetic  3.57 us (3%)
  matrix products  2.11 us (2%)
    ppermute x9, starting transfers between devices, permute(): return lax.ppermute(value, 'seq', pairs)  29.2 us
    ppermute x6, waiting for transfers between devices, shift_y(): lax.ppermute(value, 'chan', [(n, (n + by) % chans) for n in range(chans)])  15.4 us
    pallas_call x1, Pallas kernels, response_part(): pl.pallas_call(response_kernel, out_shape=jax.ShapeDtypeStruct((count * t...  15.4 us
    pallas_call x1, Pallas kernels, featurize(): pl.pallas_call(featurize_kernel, out_shape=(jax.ShapeDtypeStruct((2, rows...  13.7 us
    pallas_call x3, Pallas kernels, ends_part(): pl.pallas_call(functools.partial(ends_kernel, count=count), out_shape=jax...  10.3 us
    ppermute x6, starting transfers between devices, shift_y(): lax.ppermute(value, 'chan', [(n, (n + by) % chans) for n in range(chans)])  8.91 us
    pallas_call x1, Pallas kernels, featurize_head(): pl.pallas_call(head_kernel, out_shape=tuple((jax.ShapeDtypeStruct(v.shape...  4.08 us
    ppermute x1, starting transfers between devices, local(): halo = lax.ppermute(raw[:, -LEAD:, :], ('seq', 'chan'), following)  4.03 us
  transfers between devices with their start and end apart: 16, of which 6 were waited for; matrix products, arithmetic and copies ran while one was open for 7% of the time, Pallas kernels for 20%

profile of v1, /device:TPU:1, one launch (start us, length us, event | category | flops | bytes accessed | tf_op | source)
XLA Modules:
  0.0 118.5 jit_solution(16567179367005435132)
XLA Ops:
  1.0 4.0 %collective-permute-start = (bf16[3,8,8192]{2,1,0:T(8,128)(2,1)S(1)}, bf16[3,8,8192]{2,1,0:T(8,128)(2,1)S(1)}, u32[]{:S(2)}, u32[]{:S(2)}) collective-permute-start(bf16[3,8,8192]{2,1,0:T(8,128)(2,1)S(1)} %slice.12), channel_id=1, source_target_pairs={{0,1},{1,2},{2,3},{3,4},{4,5},{5,6},{6,7},{7,8},{8,9},{9,10},{10,1... | collective-permute-start | bytes 1179656 | tf_op jit(solution)/shard_map/ppermute | solution.py:303
  5.1 1.2 %reshape.64 = f32[21,8,8,8]{3,2,1,0:T(8,128)S(1)} reshape(f32[3,7,512]{2,1,0:T(8,128)} %param.5) | data formatting | bytes 86016 | tf_op jit(solution)/shard_map/reshape | solution.py:305
  8.1 2.1 %fusion.23 = f32[128,1344]{0,1:T(8,128)} fusion(f32[8,128]{1,0:T(8,128)S(1)} %reshape.63, f32[1344,8]{0,1:T(8,128)S(1)} %reshape.65), kind=kOutput, calls=%fused_computation.60 | convolution fusion | flops 16515072 | bytes 735232 | tf_op jit(solution)/shard_map/dot_general | solution.py:307
  10.2 13.7 %featurize.1 = (bf16[2,1024,128]{2,1,0:T(8,128)(2,1)}, bf16[2,1024,128]{2,1,0:T(8,128)(2,1)}, bf16[2,1024,128]{2,1,0:T(8,128)(2,1)}, bf16[2,1024,128]{2,1,0:T(8,...) custom-call(s32[8]{0:T(128)} %stack.64.chunks_ref, ...), custom_call_target="tpu_custom_call" | custom-call | flops 1 | bytes 1 | tf_op jit(solution)/shard_map/featurize/pallas_call | solution.py:81
  24.6 4.1 %featurize_head.1 = (bf16[2,1024,128]{2,1,0:T(8,128)(2,1)}, bf16[2,1024,128]{2,1,0:T(8,128)(2,1)}, bf16[2,1024,128]{2,1,0:T(8,128)(2,1)}, bf16[2,1024,128]{2,1,0...) custom-call(s32[8]{0:T(128)} %stack.64.chunks_ref, ...), custom_call_target="tpu_custom_call", output_to_operand_aliasing={{0}: (4, {}), {1}: (5, {}), {2}: (6, {}), {3}: (7, {}), {4}... | custom-call | flops 1 | bytes 1 | tf_op jit(solution)/shard_map/featurize_head/pallas_call | solution.py:122
  28.7 2.7 %collective-permute-start.1 = (bf16[2,1024,128]{2,1,0:T(8,128)(2,1)}, bf16[2,1024,128]{2,1,0:T(8,128)(2,1)S(1)}, u32[]{:S(2)}, u32[]{:S(2)}) collective-permute-start(bf16[2,1024,128]{2,1,0:T(8,128)(2,1)} %get-tuple-element.60), channel_id=1, source_target_pairs={{0,2},{1,3},{2,0},{3,1},{4,6},{5,7},{6,4},{7,5},{8,10},{9,11},{10,... | collective-permute-start | bytes 1572872 | tf_op jit(solution)/shard_map/ppermute | solution.py:290
  32.3 1.8 %collective-permute-start.3 = (bf16[2,1024,128]{2,1,0:T(8,128)(2,1)}, bf16[2,1024,128]{2,1,0:T(8,128)(2,1)S(1)}, u32[]{:S(2)}, u32[]{:S(2)}) collective-permute-start(bf16[2,1024,128]{2,1,0:T(8,128)(2,1)} %get-tuple-element.62), channel_id=1, source_target_pairs={{0,3},{1,0},{2,1},{3,2},{4,7},{5,4},{6,5},{7,6},{8,11},{9,8},{10,9... | collective-permute-start | bytes 1572872 | tf_op jit(solution)/shard_map/ppermute | solution.py:290
  35.0 2.9 %block_ends.5 = f32[2,128,128]{2,1,0:T(8,128)} custom-call(bf16[2,1024,128]{2,1,0:T(8,128)(2,1)} %get-tuple-element.69.refs_0_.rest_3_, f32[2,128,128]{2,1,0:T(8,128)} %get-tuple-element.86.refs_1_.refs_2_.decay_ref), custom_call_target="tpu_custom_call" | custom-call | flops 1 | bytes 1 | tf_op jit(solution)/shard_map/block_ends/pallas_call | solution.py:189
  37.8 5.2 %collective-permute-done.1.refs_0_.rest_0_ = bf16[2,1024,128]{2,1,0:T(8,128)(2,1)S(1)} collective-permute-done((bf16[2,1024,128]{2,1,0:T(8,128)(2,1)}, bf16[2,1024,128]{2,1,0:T(8,128)(2,1)S(1)}, u32[]{:S(2)}, u32[]{:S(2)}) %collective-permute-start.1) | collective-permute-done | bytes 524320 | tf_op jit(solution)/shard_map/ppermute | solution.py:290
  43.9 2.9 %block_ends.3 = f32[2,128,128]{2,1,0:T(8,128)} custom-call(bf16[2,1024,128]{2,1,0:T(8,128)(2,1)} %copy-done, f32[2,128,128]{2,1,0:T(8,128)} %get-tuple-element.86.refs_1_.refs_2_.decay_ref), custom_call_target="tpu_custom_call" | custom-call | flops 1 | bytes 1 | tf_op jit(solution)/shard_map/block_ends/pallas_call | solution.py:189
  46.7 10.2 %collective-permute-done.2.refs_0_.rest_1_ = bf16[2,1024,128]{2,1,0:T(8,128)(2,1)S(1)} collective-permute-done((bf16[2,1024,128]{2,1,0:T(8,128)(2,1)}, bf16[2,1024,128]{2,1,0:T(8,128)(2,1)S(1)}, u32[]{:S(2)}, u32[]{:S(2)}) %collective-permute-start.2) | collective-permute-done | bytes 524320 | tf_op jit(solution)/shard_map/ppermute | solution.py:290
  58.6 4.6 %block_ends.4 = f32[4,128,128]{2,1,0:T(8,128)} custom-call(bf16[2,1024,128]{2,1,0:T(8,128)(2,1)} %copy-done.1, bf16[2,1024,128]{2,1,0:T(8,128)(2,1)} %copy-done.2, f32[2,128,128]{2,1,0:T(8,128)} %get-tuple-element.86.refs_1_.refs_2_.decay_ref), custom_call_target="tpu_custom_call" | custom-call | flops 1 | bytes 1 | tf_op jit(solution)/shard_map/block_ends/pallas_call | solution.py:189
  66.0 1.3 %collective-permute-start.6 = (f32[128,128]{1,0:T(8,128)S(1)}, f32[128,128]{1,0:T(8,128)S(1)}, u32[]{:S(2)}, u32[]{:S(2)}) collective-permute-start(f32[128,128]{1,0:T(8,128)S(1)} %fusion.17), channel_id=1, source_target_pairs={{0,8},{4,12},{8,16},{12,20},{16,24},{20,28},{24,0},{28,4},{32,40},... | collective-permute-start | bytes 196616 | tf_op jit(solution)/shard_map/ppermute | solution.py:287
  67.3 2.5 %collective-permute-start.7 = (f32[128,128]{1,0:T(8,128)S(1)}, f32[128,128]{1,0:T(8,128)S(1)}, u32[]{:S(2)}, u32[]{:S(2)}) collective-permute-start(f32[128,128]{1,0:T(8,128)S(1)} %fusion.17), channel_id=1, source_target_pairs={{0,16},{4,20},{8,24},{12,28},{16,0},{20,4},{24,8},{28,12},{32,48},... | collective-permute-start | bytes 196616 | tf_op jit(solution)/shard_map/ppermute | solution.py:287
  69.7 1.2 collective-permute-start.8
  70.9 1.2 collective-permute-start.12
  72.0 2.4 %collective-permute-start.13 = (bf16[2,1024,128]{2,1,0:T(8,128)(2,1)}, bf16[2,1024,128]{2,1,0:T(8,128)(2,1)S(1)}, u32[]{:S(2)}, u32[]{:S(2)}) collective-permute-start(bf16[2,1024,128]{2,1,0:T(8,128)(2,1)} %get-tuple-element.73), channel_id=1, source_target_pairs={{0,3},{1,0},{2,1},{3,2},{4,7},{5,4},{6,5},{7,6},{8,11},{9,8},{10,9... | collective-permute-start | bytes 1572872 | tf_op jit(solution)/shard_map/ppermute | solution.py:290
  74.5 4.9 %collective-permute-start.10 = (f32[128,128]{1,0:T(8,128)S(1)}, f32[128,128]{1,0:T(8,128)S(1)}, u32[]{:S(2)}, u32[]{:S(2)}) collective-permute-start(f32[128,128]{1,0:T(8,128)S(1)} %fusion.14), channel_id=1, source_target_pairs={{0,64},{4,68},{8,72},{12,76},{16,80},{20,84},{24,88},{28,92},{32,9... | collective-permute-start | bytes 196616 | tf_op jit(solution)/shard_map/ppermute | solution.py:287
  79.4 6.6 %collective-permute-start.11 = (f32[128,128]{1,0:T(8,128)S(1)}, f32[128,128]{1,0:T(8,128)S(1)}, u32[]{:S(2)}, u32[]{:S(2)}) collective-permute-start(f32[128,128]{1,0:T(8,128)S(1)} %fusion.14), channel_id=1, source_target_pairs={{0,96},{4,100},{8,104},{12,108},{16,112},{20,116},{24,120},{28,124... | collective-permute-start | bytes 196616 | tf_op jit(solution)/shard_map/ppermute | solution.py:287
  85.9 2.6 %collective-permute-start.9 = (f32[128,128]{1,0:T(8,128)S(1)}, f32[128,128]{1,0:T(8,128)S(1)}, u32[]{:S(2)}, u32[]{:S(2)}) collective-permute-start(f32[128,128]{1,0:T(8,128)S(1)} %fusion.14), channel_id=1, source_target_pairs={{0,32},{4,36},{8,40},{12,44},{16,48},{20,52},{24,56},{28,60},{32,6... | collective-permute-start | bytes 196616 | tf_op jit(solution)/shard_map/ppermute | solution.py:287
  88.6 1.9 %collective-permute-done.9 = f32[128,128]{1,0:T(8,128)S(1)} collective-permute-done((f32[128,128]{1,0:T(8,128)S(1)}, f32[128,128]{1,0:T(8,128)S(1)}, u32[]{:S(2)}, u32[]{:S(2)}) %collective-permute-start.9) | collective-permute-done | bytes 65568 | tf_op jit(solution)/shard_map/ppermute | solution.py:287
  90.6 6.2 %collective-permute-start.14 = (f32[128,128]{1,0:T(8,128)S(1)}, f32[128,128]{1,0:T(8,128)S(1)}, u32[]{:S(2)}, u32[]{:S(2)}) collective-permute-start(f32[128,128]{1,0:T(8,128)S(1)} %get-tuple-element.74), channel_id=1, source_target_pairs={{0,128},{4,132},{8,136},{12,140},{16,144},{20,148},{24,152},{28,15... | collective-permute-start | bytes 196616 | tf_op jit(solution)/shard_map/ppermute | solution.py:287
  98.2 3.4 %collective-permute-start.15 = (f32[128,128]{1,0:T(8,128)S(1)}, f32[128,128]{1,0:T(8,128)S(1)}, u32[]{:S(2)}, u32[]{:S(2)}) collective-permute-start(f32[128,128]{1,0:T(8,128)S(1)} %get-tuple-element.79), channel_id=1, source_target_pairs={{0,4},{4,0},{8,12},{12,8},{16,20},{20,16},{24,28},{28,24},{32,36},... | collective-permute-start | bytes 196616 | tf_op jit(solution)/shard_map/ppermute | solution.py:287
  103.2 15.4 %response.1 = bf16[512,2048]{1,0:T(8,128)(2,1)} custom-call(s32[4]{0:T(128)} %pad_add_fusion.place_ref, f32[2,128,128]{2,1,0:T(8,128)} %pad_maximum_fusion.starts_ref, f32[2,128,128]{2,1,0:T(8,128)} %get-tuple-element.86.refs_1_.refs_2_.decay_ref, f32[2,128,128]{2,1,0:T(8,128)} %bitcast.157, bf16[2,1024,128]{2,1,0:T(8,128)(2,1)} %copy-done, ...), custom_call_target="tpu_custom_call" | custom-call | flops 1 | bytes 1 | tf_op jit(solution)/shard_map/response/pallas_call | solution.py:250
  (56 shorter events, 13.5 us)
Async XLA Ops:
  1.0 22.8 %collective-permute-start = (bf16[3,8,8192]{2,1,0:T(8,128)(2,1)S(1)}, bf16[3,8,8192]{2,1,0:T(8,128)(2,1)S(1)}, u32[]{:S(2)}, u32[]{:S(2)}) collective-permute-start(bf16[3,8,8192]{2,1,0:T(8,128)(2,1)S(1)} %slice.12), channel_id=1, source_target_pairs={{0,1},{1,2},{2,3},{3,4},{4,5},{5,6},{6,7},{7,8},{8,9},{9,10},{10,1... | collective-permute-start | bytes 1179656 | tf_op jit(solution)/shard_map/ppermute | solution.py:303
  23.9 10.3 %copy-start.3 = (f32[16,2048]{1,0:T(8,128)S(1)}, f32[16,2048]{1,0:T(8,128)}, u32[]{:S(2)}) copy-start(f32[16,2048]{1,0:T(8,128)} %param.6) | copy-start | bytes 393220
  28.7 68.0 %copy-start.8 = (f32[16,2048]{1,0:T(8,128)S(1)}, f32[16,2048]{1,0:T(8,128)}, u32[]{:S(2)}) copy-start(f32[16,2048]{1,0:T(8,128)} %param.7) | copy-start | bytes 393220
  28.7 14.3 %collective-permute-start.1 = (bf16[2,1024,128]{2,1,0:T(8,128)(2,1)}, bf16[2,1024,128]{2,1,0:T(8,128)(2,1)S(1)}, u32[]{:S(2)}, u32[]{:S(2)}) collective-permute-start(bf16[2,1024,128]{2,1,0:T(8,128)(2,1)} %get-tuple-element.60), channel_id=1, source_target_pairs={{0,2},{1,3},{2,0},{3,1},{4,6},{5,7},{6,4},{7,5},{8,10},{9,11},{10,... | collective-permute-start | bytes 1572872 | tf_op jit(solution)/shard_map/ppermute | solution.py:290
  31.4 25.5 %collective-permute-start.2 = (bf16[2,1024,128]{2,1,0:T(8,128)(2,1)}, bf16[2,1024,128]{2,1,0:T(8,128)(2,1)S(1)}, u32[]{:S(2)}, u32[]{:S(2)}) collective-permute-start(bf16[2,1024,128]{2,1,0:T(8,128)(2,1)} %get-tuple-element.61), channel_id=1, source_target_pairs={{0,1},{1,2},{2,3},{3,0},{4,5},{5,6},{6,7},{7,4},{8,9},{9,10},{10,1... | collective-permute-start | bytes 1572872 | tf_op jit(solution)/shard_map/ppermute | solution.py:290
  32.3 24.7 %collective-permute-start.3 = (bf16[2,1024,128]{2,1,0:T(8,128)(2,1)}, bf16[2,1024,128]{2,1,0:T(8,128)(2,1)S(1)}, u32[]{:S(2)}, u32[]{:S(2)}) collective-permute-start(bf16[2,1024,128]{2,1,0:T(8,128)(2,1)} %get-tuple-element.62), channel_id=1, source_target_pairs={{0,3},{1,0},{2,1},{3,2},{4,7},{5,4},{6,5},{7,6},{8,11},{9,8},{10,9... | collective-permute-start | bytes 1572872 | tf_op jit(solution)/shard_map/ppermute | solution.py:290
  35.0 31.0 %collective-permute-start.5 = (bf16[2,1024,128]{2,1,0:T(8,128)(2,1)}, bf16[2,1024,128]{2,1,0:T(8,128)(2,1)S(1)}, u32[]{:S(2)}, u32[]{:S(2)}) collective-permute-start(bf16[2,1024,128]{2,1,0:T(8,128)(2,1)} %get-tuple-element.70), channel_id=1, source_target_pairs={{0,2},{1,3},{2,0},{3,1},{4,6},{5,7},{6,4},{7,5},{8,10},{9,11},{10,... | collective-permute-start | bytes 1572872 | tf_op jit(solution)/shard_map/ppermute | solution.py:290
  43.0 0.8 copy-start
  57.0 0.8 copy-start.1
  57.8 0.8 copy-start.2
  64.4 1.6 %collective-permute-start.4 = (f32[128,128]{1,0:T(8,128)S(1)}, f32[128,128]{1,0:T(8,128)S(1)}, u32[]{:S(2)}, u32[]{:S(2)}) collective-permute-start(f32[128,128]{1,0:T(8,128)S(1)} %dynamic-slice_bitcast_fusion), channel_id=1, source_target_pairs={{0,4},{4,0},{8,12},{12,8},{16,20},{20,16},{24,28},{28,24},{32,36},... | collective-permute-start | bytes 196616 | tf_op jit(solution)/shard_map/ppermute | solution.py:287
  66.0 37.2 %copy-start.4 = (bf16[2,1024,128]{2,1,0:T(8,128)(2,1)}, bf16[2,1024,128]{2,1,0:T(8,128)(2,1)S(1)}, u32[]{:S(2)}) copy-start(bf16[2,1024,128]{2,1,0:T(8,128)(2,1)S(1)} %collective-permute-done.5.rest_4_) | copy-start | bytes 1572868
  66.0 8.4 %collective-permute-start.6 = (f32[128,128]{1,0:T(8,128)S(1)}, f32[128,128]{1,0:T(8,128)S(1)}, u32[]{:S(2)}, u32[]{:S(2)}) collective-permute-start(f32[128,128]{1,0:T(8,128)S(1)} %fusion.17), channel_id=1, source_target_pairs={{0,8},{4,12},{8,16},{12,20},{16,24},{20,28},{24,0},{28,4},{32,40},... | collective-permute-start | bytes 196616 | tf_op jit(solution)/shard_map/ppermute | solution.py:287
  67.3 7.1 %collective-permute-start.7 = (f32[128,128]{1,0:T(8,128)S(1)}, f32[128,128]{1,0:T(8,128)S(1)}, u32[]{:S(2)}, u32[]{:S(2)}) collective-permute-start(f32[128,128]{1,0:T(8,128)S(1)} %fusion.17), channel_id=1, source_target_pairs={{0,16},{4,20},{8,24},{12,28},{16,0},{20,4},{24,8},{28,12},{32,48},... | collective-permute-start | bytes 196616 | tf_op jit(solution)/shard_map/ppermute | solution.py:287
  69.7 4.7 %collective-permute-start.8 = (f32[128,128]{1,0:T(8,128)S(1)}, f32[128,128]{1,0:T(8,128)S(1)}, u32[]{:S(2)}, u32[]{:S(2)}) collective-permute-start(f32[128,128]{1,0:T(8,128)S(1)} %fusion.17), channel_id=1, source_target_pairs={{0,24},{4,28},{8,0},{12,4},{16,8},{20,12},{24,16},{28,20},{32,56},... | collective-permute-start | bytes 196616 | tf_op jit(solution)/shard_map/ppermute | solution.py:287
  70.9 19.7 %collective-permute-start.12 = (bf16[2,1024,128]{2,1,0:T(8,128)(2,1)}, bf16[2,1024,128]{2,1,0:T(8,128)(2,1)S(1)}, u32[]{:S(2)}, u32[]{:S(2)}) collective-permute-start(bf16[2,1024,128]{2,1,0:T(8,128)(2,1)} %get-tuple-element.72), channel_id=1, source_target_pairs={{0,1},{1,2},{2,3},{3,0},{4,5},{5,6},{6,7},{7,4},{8,9},{9,10},{10,1... | collective-permute-start | bytes 1572872 | tf_op jit(solution)/shard_map/ppermute | solution.py:290
  72.0 18.5 %collective-permute-start.13 = (bf16[2,1024,128]{2,1,0:T(8,128)(2,1)}, bf16[2,1024,128]{2,1,0:T(8,128)(2,1)S(1)}, u32[]{:S(2)}, u32[]{:S(2)}) collective-permute-start(bf16[2,1024,128]{2,1,0:T(8,128)(2,1)} %get-tuple-element.73), channel_id=1, source_target_pairs={{0,3},{1,0},{2,1},{3,2},{4,7},{5,4},{6,5},{7,6},{8,11},{9,8},{10,9... | collective-permute-start | bytes 1572872 | tf_op jit(solution)/shard_map/ppermute | solution.py:290
  74.5 14.1 %collective-permute-start.10 = (f32[128,128]{1,0:T(8,128)S(1)}, f32[128,128]{1,0:T(8,128)S(1)}, u32[]{:S(2)}, u32[]{:S(2)}) collective-permute-start(f32[128,128]{1,0:T(8,128)S(1)} %fusion.14), channel_id=1, source_target_pairs={{0,64},{4,68},{8,72},{12,76},{16,80},{20,84},{24,88},{28,92},{32,9... | collective-permute-start | bytes 196616 | tf_op jit(solution)/shard_map/ppermute | solution.py:287
  79.4 9.2 %collective-permute-start.11 = (f32[128,128]{1,0:T(8,128)S(1)}, f32[128,128]{1,0:T(8,128)S(1)}, u32[]{:S(2)}, u32[]{:S(2)}) collective-permute-start(f32[128,128]{1,0:T(8,128)S(1)} %fusion.14), channel_id=1, source_target_pairs={{0,96},{4,100},{8,104},{12,108},{16,112},{20,116},{24,120},{28,124... | collective-permute-start | bytes 196616 | tf_op jit(solution)/shard_map/ppermute | solution.py:287
  85.9 4.5 %collective-permute-start.9 = (f32[128,128]{1,0:T(8,128)S(1)}, f32[128,128]{1,0:T(8,128)S(1)}, u32[]{:S(2)}, u32[]{:S(2)}) collective-permute-start(f32[128,128]{1,0:T(8,128)S(1)} %fusion.14), channel_id=1, source_target_pairs={{0,32},{4,36},{8,40},{12,44},{16,48},{20,52},{24,56},{28,60},{32,6... | collective-permute-start | bytes 196616 | tf_op jit(solution)/shard_map/ppermute | solution.py:287
  90.5 12.6 %copy-start.5 = (bf16[2,1024,128]{2,1,0:T(8,128)(2,1)}, bf16[2,1024,128]{2,1,0:T(8,128)(2,1)S(1)}, u32[]{:S(2)}) copy-start(bf16[2,1024,128]{2,1,0:T(8,128)(2,1)S(1)} %collective-permute-done.12.rest_5_) | copy-start | bytes 1572868
  90.6 12.6 %copy-start.6 = (bf16[2,1024,128]{2,1,0:T(8,128)(2,1)}, bf16[2,1024,128]{2,1,0:T(8,128)(2,1)S(1)}, u32[]{:S(2)}) copy-start(bf16[2,1024,128]{2,1,0:T(8,128)(2,1)S(1)} %collective-permute-done.13.rest_6_) | copy-start | bytes 1572868
  90.6 7.5 %collective-permute-start.14 = (f32[128,128]{1,0:T(8,128)S(1)}, f32[128,128]{1,0:T(8,128)S(1)}, u32[]{:S(2)}, u32[]{:S(2)}) collective-permute-start(f32[128,128]{1,0:T(8,128)S(1)} %get-tuple-element.74), channel_id=1, source_target_pairs={{0,128},{4,132},{8,136},{12,140},{16,144},{20,148},{24,152},{28,15... | collective-permute-start | bytes 196616 | tf_op jit(solution)/shard_map/ppermute | solution.py:287
  98.2 4.3 %collective-permute-start.15 = (f32[128,128]{1,0:T(8,128)S(1)}, f32[128,128]{1,0:T(8,128)S(1)}, u32[]{:S(2)}, u32[]{:S(2)}) collective-permute-start(f32[128,128]{1,0:T(8,128)S(1)} %get-tuple-element.79), channel_id=1, source_target_pairs={{0,4},{4,0},{8,12},{12,8},{16,20},{20,16},{24,28},{28,24},{32,36},... | collective-permute-start | bytes 196616 | tf_op jit(solution)/shard_map/ppermute | solution.py:287
  (1 other events, 0.8 us)

commit v2 on v1

--- a/solution.py
+++ b/solution.py
@@ -300,13 +300,14 @@
 
     raw = jnp.transpose(qkv, (1, 0, 2))
     following = [(n, n + 1) for n in range(seqs * chans - 1)]
-    halo = lax.ppermute(raw[:, -LEAD:, :], ("seq", "chan"), following)
 
     small = jnp.transpose(short_filter.reshape(3 * TAPS, -1, SUB, LANES // GROUP), (1, 0, 2, 3))
     spread = jnp.repeat(jnp.eye(LANES // GROUP, dtype=F32), GROUP, axis=1)
     taps = jnp.dot(
         small.reshape(-1, LANES // GROUP), spread, precision=lax.Precision.HIGHEST
     ).reshape(-1, 3 * TAPS * SUB, LANES)
+    last_rows, taps = lax.optimization_barrier((raw[:, -LEAD:, :], taps))
+    halo = lax.ppermute(last_rows, ("seq", "chan"), following)
 
     def chunked(value):
         pieces = jnp.transpose(value.reshape(MODES, 2, SUB, LANES), (1, 0, 2, 3))

time: 119 us -> 119 us (level)
  transfers between devices with their start and end apart: 16 -> 16, of which waited for: 6 -> 6; matrix products, arithmetic and copies ran while one was open for 7% -> 4% of each run, Pallas kernels for 20% -> 20%
where the time goes in v2:
time: 119 us
  Pallas kernels  43.5 us (37%)
  starting transfers between devices  42.2 us (35%)
  waiting for transfers between devices  19 us (16%)
  local copies, waits for them, and re-layouts  7.91 us (7%)
  other arithmetic  3.57 us (3%)
  matrix products  2.12 us (2%)
    ppermute x9, starting transfers between devices, permute(): return lax.ppermute(value, 'seq', pairs)  29.2 us
    ppermute x6, waiting for transfers between devices, shift_y(): lax.ppermute(value, 'chan', [(n, (n + by) % chans) for n in range(chans)])  15.4 us
    pallas_call x1, Pallas kernels, response_part(): pl.pallas_call(response_kernel, out_shape=jax.ShapeDtypeStruct((count * t...  15.4 us
    pallas_call x1, Pallas kernels, featurize(): pl.pallas_call(featurize_kernel, out_shape=(jax.ShapeDtypeStruct((2, rows...  13.7 us
    pallas_call x3, Pallas kernels, ends_part(): pl.pallas_call(functools.partial(ends_kernel, count=count), out_shape=jax...  10.3 us
    ppermute x6, starting transfers between devices, shift_y(): lax.ppermute(value, 'chan', [(n, (n + by) % chans) for n in range(chans)])  8.91 us
    pallas_call x1, Pallas kernels, featurize_head(): pl.pallas_call(head_kernel, out_shape=tuple((jax.ShapeDtypeStruct(v.shape...  4.08 us
    ppermute x1, starting transfers between devices, local(): halo = lax.ppermute(last_rows, ('seq', 'chan'), following)  4.02 us
  transfers between devices with their start and end apart: 16, of which 6 were waited for; matrix products, arithmetic and copies ran while one was open for 4% of the time, Pallas kernels for 20%

profile of v2, /device:TPU:1, one launch (start us, length us, event | category | flops | bytes accessed | tf_op | source)
XLA Modules:
  0.0 118.5 jit_solution(9106931006618192128)
XLA Ops:
  1.0 1.2 %reshape.64 = f32[21,8,8,8]{3,2,1,0:T(8,128)S(1)} reshape(f32[3,7,512]{2,1,0:T(8,128)} %param.5) | data formatting | bytes 86016 | tf_op jit(solution)/shard_map/reshape | solution.py:304
  3.3 2.1 %fusion.23 = f32[128,1344]{0,1:T(8,128)} fusion(f32[8,128]{1,0:T(8,128)S(1)} %reshape.63, f32[1344,8]{0,1:T(8,128)S(1)} %reshape.65), kind=kOutput, calls=%fused_computation.60 | convolution fusion | flops 16515072 | bytes 735232 | tf_op jit(solution)/shard_map/dot_general | solution.py:306
  5.5 4.0 %collective-permute-start = (bf16[3,8,8192]{2,1,0:T(8,128)(2,1)S(1)}, bf16[3,8,8192]{2,1,0:T(8,128)(2,1)S(1)}, u32[]{:S(2)}, u32[]{:S(2)}) collective-permute-start(bf16[3,8,8192]{2,1,0:T(8,128)(2,1)S(1)} %slice.12), channel_id=1, source_target_pairs={{0,1},{1,2},{2,3},{3,4},{4,5},{5,6},{6,7},{7,8},{8,9},{9,10},{10,1... | collective-permute-start | bytes 1179656 | tf_op jit(solution)/shard_map/ppermute | solution.py:310
  10.2 13.7 %featurize.1 = (bf16[2,1024,128]{2,1,0:T(8,128)(2,1)}, bf16[2,1024,128]{2,1,0:T(8,128)(2,1)}, bf16[2,1024,128]{2,1,0:T(8,128)(2,1)}, bf16[2,1024,128]{2,1,0:T(8,...) custom-call(s32[8]{0:T(128)} %stack.64.chunks_ref, ...), custom_call_target="tpu_custom_call" | custom-call | flops 1 | bytes 1 | tf_op jit(solution)/shard_map/featurize/pallas_call | solution.py:81
  24.6 4.1 %featurize_head.1 = (bf16[2,1024,128]{2,1,0:T(8,128)(2,1)}, bf16[2,1024,128]{2,1,0:T(8,128)(2,1)}, bf16[2,1024,128]{2,1,0:T(8,128)(2,1)}, bf16[2,1024,128]{2,1,0...) custom-call(s32[8]{0:T(128)} %stack.64.chunks_ref, ...), custom_call_target="tpu_custom_call", output_to_operand_aliasing={{0}: (4, {}), {1}: (5, {}), {2}: (6, {}), {3}: (7, {}), {4}... | custom-call | flops 1 | bytes 1 | tf_op jit(solution)/shard_map/featurize_head/pallas_call | solution.py:122
  28.7 2.7 %collective-permute-start.1 = (bf16[2,1024,128]{2,1,0:T(8,128)(2,1)}, bf16[2,1024,128]{2,1,0:T(8,128)(2,1)S(1)}, u32[]{:S(2)}, u32[]{:S(2)}) collective-permute-start(bf16[2,1024,128]{2,1,0:T(8,128)(2,1)} %get-tuple-element.64), channel_id=1, source_target_pairs={{0,2},{1,3},{2,0},{3,1},{4,6},{5,7},{6,4},{7,5},{8,10},{9,11},{10,... | collective-permute-start | bytes 1572872 | tf_op jit(solution)/shard_map/ppermute | solution.py:290
  32.3 1.8 %collective-permute-start.3 = (bf16[2,1024,128]{2,1,0:T(8,128)(2,1)}, bf16[2,1024,128]{2,1,0:T(8,128)(2,1)S(1)}, u32[]{:S(2)}, u32[]{:S(2)}) collective-permute-start(bf16[2,1024,128]{2,1,0:T(8,128)(2,1)} %get-tuple-element.66), channel_id=1, source_target_pairs={{0,3},{1,0},{2,1},{3,2},{4,7},{5,4},{6,5},{7,6},{8,11},{9,8},{10,9... | collective-permute-start | bytes 1572872 | tf_op jit(solution)/shard_map/ppermute | solution.py:290
  34.9 2.9 %block_ends.5 = f32[2,128,128]{2,1,0:T(8,128)} custom-call(bf16[2,1024,128]{2,1,0:T(8,128)(2,1)} %get-tuple-element.73.refs_0_.rest_3_, f32[2,128,128]{2,1,0:T(8,128)} %get-tuple-element.90.refs_1_.refs_2_.decay_ref), custom_call_target="tpu_custom_call" | custom-call | flops 1 | bytes 1 | tf_op jit(solution)/shard_map/block_ends/pallas_call | solution.py:189
  37.8 5.2 %collective-permute-done.1.refs_0_.rest_0_ = bf16[2,1024,128]{2,1,0:T(8,128)(2,1)S(1)} collective-permute-done((bf16[2,1024,128]{2,1,0:T(8,128)(2,1)}, bf16[2,1024,128]{2,1,0:T(8,128)(2,1)S(1)}, u32[]{:S(2)}, u32[]{:S(2)}) %collective-permute-start.1) | collective-permute-done | bytes 524320 | tf_op jit(solution)/shard_map/ppermute | solution.py:290
  43.8 2.9 %block_ends.3 = f32[2,128,128]{2,1,0:T(8,128)} custom-call(bf16[2,1024,128]{2,1,0:T(8,128)(2,1)} %copy-done, f32[2,128,128]{2,1,0:T(8,128)} %get-tuple-element.90.refs_1_.refs_2_.decay_ref), custom_call_target="tpu_custom_call" | custom-call | flops 1 | bytes 1 | tf_op jit(solution)/shard_map/block_ends/pallas_call | solution.py:189
  46.7 10.2 %collective-permute-done.2.refs_0_.rest_1_ = bf16[2,1024,128]{2,1,0:T(8,128)(2,1)S(1)} collective-permute-done((bf16[2,1024,128]{2,1,0:T(8,128)(2,1)}, bf16[2,1024,128]{2,1,0:T(8,128)(2,1)S(1)}, u32[]{:S(2)}, u32[]{:S(2)}) %collective-permute-start.2) | collective-permute-done | bytes 524320 | tf_op jit(solution)/shard_map/ppermute | solution.py:290
  58.6 4.6 %block_ends.4 = f32[4,128,128]{2,1,0:T(8,128)} custom-call(bf16[2,1024,128]{2,1,0:T(8,128)(2,1)} %copy-done.1, bf16[2,1024,128]{2,1,0:T(8,128)(2,1)} %copy-done.2, f32[2,128,128]{2,1,0:T(8,128)} %get-tuple-element.90.refs_1_.refs_2_.decay_ref), custom_call_target="tpu_custom_call" | custom-call | flops 1 | bytes 1 | tf_op jit(solution)/shard_map/block_ends/pallas_call | solution.py:189
  66.0 1.3 %collective-permute-start.6 = (f32[128,128]{1,0:T(8,128)S(1)}, f32[128,128]{1,0:T(8,128)S(1)}, u32[]{:S(2)}, u32[]{:S(2)}) collective-permute-start(f32[128,128]{1,0:T(8,128)S(1)} %fusion.17), channel_id=1, source_target_pairs={{0,8},{4,12},{8,16},{12,20},{16,24},{20,28},{24,0},{28,4},{32,40},... | collective-permute-start | bytes 196616 | tf_op jit(solution)/shard_map/ppermute | solution.py:287
  67.2 2.5 %collective-permute-start.7 = (f32[128,128]{1,0:T(8,128)S(1)}, f32[128,128]{1,0:T(8,128)S(1)}, u32[]{:S(2)}, u32[]{:S(2)}) collective-permute-start(f32[128,128]{1,0:T(8,128)S(1)} %fusion.17), channel_id=1, source_target_pairs={{0,16},{4,20},{8,24},{12,28},{16,0},{20,4},{24,8},{28,12},{32,48},... | collective-permute-start | bytes 196616 | tf_op jit(solution)/shard_map/ppermute | solution.py:287
  69.7 1.2 collective-permute-start.8
  70.8 1.2 collective-permute-start.12
  72.0 2.4 %collective-permute-start.13 = (bf16[2,1024,128]{2,1,0:T(8,128)(2,1)}, bf16[2,1024,128]{2,1,0:T(8,128)(2,1)S(1)}, u32[]{:S(2)}, u32[]{:S(2)}) collective-permute-start(bf16[2,1024,128]{2,1,0:T(8,128)(2,1)} %get-tuple-element.77), channel_id=1, source_target_pairs={{0,3},{1,0},{2,1},{3,2},{4,7},{5,4},{6,5},{7,6},{8,11},{9,8},{10,9... | collective-permute-start | bytes 1572872 | tf_op jit(solution)/shard_map/ppermute | solution.py:290
  74.4 4.9 %collective-permute-start.10 = (f32[128,128]{1,0:T(8,128)S(1)}, f32[128,128]{1,0:T(8,128)S(1)}, u32[]{:S(2)}, u32[]{:S(2)}) collective-permute-start(f32[128,128]{1,0:T(8,128)S(1)} %fusion.14), channel_id=1, source_target_pairs={{0,64},{4,68},{8,72},{12,76},{16,80},{20,84},{24,88},{28,92},{32,9... | collective-permute-start | bytes 196616 | tf_op jit(solution)/shard_map/ppermute | solution.py:287
  79.4 6.6 %collective-permute-start.11 = (f32[128,128]{1,0:T(8,128)S(1)}, f32[128,128]{1,0:T(8,128)S(1)}, u32[]{:S(2)}, u32[]{:S(2)}) collective-permute-start(f32[128,128]{1,0:T(8,128)S(1)} %fusion.14), channel_id=1, source_target_pairs={{0,96},{4,100},{8,104},{12,108},{16,112},{20,116},{24,120},{28,124... | collective-permute-start | bytes 196616 | tf_op jit(solution)/shard_map/ppermute | solution.py:287
  85.9 2.6 %collective-permute-start.9 = (f32[128,128]{1,0:T(8,128)S(1)}, f32[128,128]{1,0:T(8,128)S(1)}, u32[]{:S(2)}, u32[]{:S(2)}) collective-permute-start(f32[128,128]{1,0:T(8,128)S(1)} %fusion.14), channel_id=1, source_target_pairs={{0,32},{4,36},{8,40},{12,44},{16,48},{20,52},{24,56},{28,60},{32,6... | collective-permute-start | bytes 196616 | tf_op jit(solution)/shard_map/ppermute | solution.py:287
  88.6 1.9 %collective-permute-done.9 = f32[128,128]{1,0:T(8,128)S(1)} collective-permute-done((f32[128,128]{1,0:T(8,128)S(1)}, f32[128,128]{1,0:T(8,128)S(1)}, u32[]{:S(2)}, u32[]{:S(2)}) %collective-permute-start.9) | collective-permute-done | bytes 65568 | tf_op jit(solution)/shard_map/ppermute | solution.py:287
  90.6 6.2 %collective-permute-start.14 = (f32[128,128]{1,0:T(8,128)S(1)}, f32[128,128]{1,0:T(8,128)S(1)}, u32[]{:S(2)}, u32[]{:S(2)}) collective-permute-start(f32[128,128]{1,0:T(8,128)S(1)} %get-tuple-element.78), channel_id=1, source_target_pairs={{0,128},{4,132},{8,136},{12,140},{16,144},{20,148},{24,152},{28,15... | collective-permute-start | bytes 196616 | tf_op jit(solution)/shard_map/ppermute | solution.py:287
  98.2 3.4 %collective-permute-start.15 = (f32[128,128]{1,0:T(8,128)S(1)}, f32[128,128]{1,0:T(8,128)S(1)}, u32[]{:S(2)}, u32[]{:S(2)}) collective-permute-start(f32[128,128]{1,0:T(8,128)S(1)} %get-tuple-element.83), channel_id=1, source_target_pairs={{0,4},{4,0},{8,12},{12,8},{16,20},{20,16},{24,28},{28,24},{32,36},... | collective-permute-start | bytes 196616 | tf_op jit(solution)/shard_map/ppermute | solution.py:287
  103.1 15.4 %response.1 = bf16[512,2048]{1,0:T(8,128)(2,1)} custom-call(s32[4]{0:T(128)} %pad_add_fusion.place_ref, f32[2,128,128]{2,1,0:T(8,128)} %pad_maximum_fusion.starts_ref, f32[2,128,128]{2,1,0:T(8,128)} %get-tuple-element.90.refs_1_.refs_2_.decay_ref, f32[2,128,128]{2,1,0:T(8,128)} %bitcast.157, bf16[2,1024,128]{2,1,0:T(8,128)(2,1)} %copy-done, ...), custom_call_target="tpu_custom_call" | custom-call | flops 1 | bytes 1 | tf_op jit(solution)/shard_map/response/pallas_call | solution.py:250
  (56 shorter events, 13.5 us)
Async XLA Ops:
  5.5 18.4 %collective-permute-start = (bf16[3,8,8192]{2,1,0:T(8,128)(2,1)S(1)}, bf16[3,8,8192]{2,1,0:T(8,128)(2,1)S(1)}, u32[]{:S(2)}, u32[]{:S(2)}) collective-permute-start(bf16[3,8,8192]{2,1,0:T(8,128)(2,1)S(1)} %slice.12), channel_id=1, source_target_pairs={{0,1},{1,2},{2,3},{3,4},{4,5},{5,6},{6,7},{7,8},{8,9},{9,10},{10,1... | collective-permute-start | bytes 1179656 | tf_op jit(solution)/shard_map/ppermute | solution.py:310
  23.8 10.3 %copy-start.3 = (f32[16,2048]{1,0:T(8,128)S(1)}, f32[16,2048]{1,0:T(8,128)}, u32[]{:S(2)}) copy-start(f32[16,2048]{1,0:T(8,128)} %param.6) | copy-start | bytes 393220
  28.7 68.0 %copy-start.8 = (f32[16,2048]{1,0:T(8,128)S(1)}, f32[16,2048]{1,0:T(8,128)}, u32[]{:S(2)}) copy-start(f32[16,2048]{1,0:T(8,128)} %param.7) | copy-start | bytes 393220
  28.7 14.3 %collective-permute-start.1 = (bf16[2,1024,128]{2,1,0:T(8,128)(2,1)}, bf16[2,1024,128]{2,1,0:T(8,128)(2,1)S(1)}, u32[]{:S(2)}, u32[]{:S(2)}) collective-permute-start(bf16[2,1024,128]{2,1,0:T(8,128)(2,1)} %get-tuple-element.64), channel_id=1, source_target_pairs={{0,2},{1,3},{2,0},{3,1},{4,6},{5,7},{6,4},{7,5},{8,10},{9,11},{10,... | collective-permute-start | bytes 1572872 | tf_op jit(solution)/shard_map/ppermute | solution.py:290
  31.4 25.5 %collective-permute-start.2 = (bf16[2,1024,128]{2,1,0:T(8,128)(2,1)}, bf16[2,1024,128]{2,1,0:T(8,128)(2,1)S(1)}, u32[]{:S(2)}, u32[]{:S(2)}) collective-permute-start(bf16[2,1024,128]{2,1,0:T(8,128)(2,1)} %get-tuple-element.65), channel_id=1, source_target_pairs={{0,1},{1,2},{2,3},{3,0},{4,5},{5,6},{6,7},{7,4},{8,9},{9,10},{10,1... | collective-permute-start | bytes 1572872 | tf_op jit(solution)/shard_map/ppermute | solution.py:290
  32.3 24.7 %collective-permute-start.3 = (bf16[2,1024,128]{2,1,0:T(8,128)(2,1)}, bf16[2,1024,128]{2,1,0:T(8,128)(2,1)S(1)}, u32[]{:S(2)}, u32[]{:S(2)}) collective-permute-start(bf16[2,1024,128]{2,1,0:T(8,128)(2,1)} %get-tuple-element.66), channel_id=1, source_target_pairs={{0,3},{1,0},{2,1},{3,2},{4,7},{5,4},{6,5},{7,6},{8,11},{9,8},{10,9... | collective-permute-start | bytes 1572872 | tf_op jit(solution)/shard_map/ppermute | solution.py:290
  34.9 31.0 %collective-permute-start.5 = (bf16[2,1024,128]{2,1,0:T(8,128)(2,1)}, bf16[2,1024,128]{2,1,0:T(8,128)(2,1)S(1)}, u32[]{:S(2)}, u32[]{:S(2)}) collective-permute-start(bf16[2,1024,128]{2,1,0:T(8,128)(2,1)} %get-tuple-element.74), channel_id=1, source_target_pairs={{0,2},{1,3},{2,0},{3,1},{4,6},{5,7},{6,4},{7,5},{8,10},{9,11},{10,... | collective-permute-start | bytes 1572872 | tf_op jit(solution)/shard_map/ppermute | solution.py:290
  43.0 0.8 copy-start
  57.0 0.8 copy-start.1
  57.8 0.8 copy-start.2
  64.3 1.6 %collective-permute-start.4 = (f32[128,128]{1,0:T(8,128)S(1)}, f32[128,128]{1,0:T(8,128)S(1)}, u32[]{:S(2)}, u32[]{:S(2)}) collective-permute-start(f32[128,128]{1,0:T(8,128)S(1)} %dynamic-slice_bitcast_fusion), channel_id=1, source_target_pairs={{0,4},{4,0},{8,12},{12,8},{16,20},{20,16},{24,28},{28,24},{32,36},... | collective-permute-start | bytes 196616 | tf_op jit(solution)/shard_map/ppermute | solution.py:287
  66.0 37.2 %copy-start.4 = (bf16[2,1024,128]{2,1,0:T(8,128)(2,1)}, bf16[2,1024,128]{2,1,0:T(8,128)(2,1)S(1)}, u32[]{:S(2)}) copy-start(bf16[2,1024,128]{2,1,0:T(8,128)(2,1)S(1)} %collective-permute-done.5.rest_4_) | copy-start | bytes 1572868
  66.0 8.4 %collective-permute-start.6 = (f32[128,128]{1,0:T(8,128)S(1)}, f32[128,128]{1,0:T(8,128)S(1)}, u32[]{:S(2)}, u32[]{:S(2)}) collective-permute-start(f32[128,128]{1,0:T(8,128)S(1)} %fusion.17), channel_id=1, source_target_pairs={{0,8},{4,12},{8,16},{12,20},{16,24},{20,28},{24,0},{28,4},{32,40},... | collective-permute-start | bytes 196616 | tf_op jit(solution)/shard_map/ppermute | solution.py:287
  67.2 7.1 %collective-permute-start.7 = (f32[128,128]{1,0:T(8,128)S(1)}, f32[128,128]{1,0:T(8,128)S(1)}, u32[]{:S(2)}, u32[]{:S(2)}) collective-permute-start(f32[128,128]{1,0:T(8,128)S(1)} %fusion.17), channel_id=1, source_target_pairs={{0,16},{4,20},{8,24},{12,28},{16,0},{20,4},{24,8},{28,12},{32,48},... | collective-permute-start | bytes 196616 | tf_op jit(solution)/shard_map/ppermute | solution.py:287
  69.7 4.7 %collective-permute-start.8 = (f32[128,128]{1,0:T(8,128)S(1)}, f32[128,128]{1,0:T(8,128)S(1)}, u32[]{:S(2)}, u32[]{:S(2)}) collective-permute-start(f32[128,128]{1,0:T(8,128)S(1)} %fusion.17), channel_id=1, source_target_pairs={{0,24},{4,28},{8,0},{12,4},{16,8},{20,12},{24,16},{28,20},{32,56},... | collective-permute-start | bytes 196616 | tf_op jit(solution)/shard_map/ppermute | solution.py:287
  70.8 19.7 %collective-permute-start.12 = (bf16[2,1024,128]{2,1,0:T(8,128)(2,1)}, bf16[2,1024,128]{2,1,0:T(8,128)(2,1)S(1)}, u32[]{:S(2)}, u32[]{:S(2)}) collective-permute-start(bf16[2,1024,128]{2,1,0:T(8,128)(2,1)} %get-tuple-element.76), channel_id=1, source_target_pairs={{0,1},{1,2},{2,3},{3,0},{4,5},{5,6},{6,7},{7,4},{8,9},{9,10},{10,1... | collective-permute-start | bytes 1572872 | tf_op jit(solution)/shard_map/ppermute | solution.py:290
  72.0 18.5 %collective-permute-start.13 = (bf16[2,1024,128]{2,1,0:T(8,128)(2,1)}, bf16[2,1024,128]{2,1,0:T(8,128)(2,1)S(1)}, u32[]{:S(2)}, u32[]{:S(2)}) collective-permute-start(bf16[2,1024,128]{2,1,0:T(8,128)(2,1)} %get-tuple-element.77), channel_id=1, source_target_pairs={{0,3},{1,0},{2,1},{3,2},{4,7},{5,4},{6,5},{7,6},{8,11},{9,8},{10,9... | collective-permute-start | bytes 1572872 | tf_op jit(solution)/shard_map/ppermute | solution.py:290
  74.4 14.1 %collective-permute-start.10 = (f32[128,128]{1,0:T(8,128)S(1)}, f32[128,128]{1,0:T(8,128)S(1)}, u32[]{:S(2)}, u32[]{:S(2)}) collective-permute-start(f32[128,128]{1,0:T(8,128)S(1)} %fusion.14), channel_id=1, source_target_pairs={{0,64},{4,68},{8,72},{12,76},{16,80},{20,84},{24,88},{28,92},{32,9... | collective-permute-start | bytes 196616 | tf_op jit(solution)/shard_map/ppermute | solution.py:287
  79.4 9.2 %collective-permute-start.11 = (f32[128,128]{1,0:T(8,128)S(1)}, f32[128,128]{1,0:T(8,128)S(1)}, u32[]{:S(2)}, u32[]{:S(2)}) collective-permute-start(f32[128,128]{1,0:T(8,128)S(1)} %fusion.14), channel_id=1, source_target_pairs={{0,96},{4,100},{8,104},{12,108},{16,112},{20,116},{24,120},{28,124... | collective-permute-start | bytes 196616 | tf_op jit(solution)/shard_map/ppermute | solution.py:287
  85.9 4.5 %collective-permute-start.9 = (f32[128,128]{1,0:T(8,128)S(1)}, f32[128,128]{1,0:T(8,128)S(1)}, u32[]{:S(2)}, u32[]{:S(2)}) collective-permute-start(f32[128,128]{1,0:T(8,128)S(1)} %fusion.14), channel_id=1, source_target_pairs={{0,32},{4,36},{8,40},{12,44},{16,48},{20,52},{24,56},{28,60},{32,6... | collective-permute-start | bytes 196616 | tf_op jit(solution)/shard_map/ppermute | solution.py:287
  90.5 12.6 %copy-start.5 = (bf16[2,1024,128]{2,1,0:T(8,128)(2,1)}, bf16[2,1024,128]{2,1,0:T(8,128)(2,1)S(1)}, u32[]{:S(2)}) copy-start(bf16[2,1024,128]{2,1,0:T(8,128)(2,1)S(1)} %collective-permute-done.12.rest_5_) | copy-start | bytes 1572868
  90.5 12.6 %copy-start.6 = (bf16[2,1024,128]{2,1,0:T(8,128)(2,1)}, bf16[2,1024,128]{2,1,0:T(8,128)(2,1)S(1)}, u32[]{:S(2)}) copy-start(bf16[2,1024,128]{2,1,0:T(8,128)(2,1)S(1)} %collective-permute-done.13.rest_6_) | copy-start | bytes 1572868
  90.6 7.5 %collective-permute-start.14 = (f32[128,128]{1,0:T(8,128)S(1)}, f32[128,128]{1,0:T(8,128)S(1)}, u32[]{:S(2)}, u32[]{:S(2)}) collective-permute-start(f32[128,128]{1,0:T(8,128)S(1)} %get-tuple-element.78), channel_id=1, source_target_pairs={{0,128},{4,132},{8,136},{12,140},{16,144},{20,148},{24,152},{28,15... | collective-permute-start | bytes 196616 | tf_op jit(solution)/shard_map/ppermute | solution.py:287
  98.2 4.3 %collective-permute-start.15 = (f32[128,128]{1,0:T(8,128)S(1)}, f32[128,128]{1,0:T(8,128)S(1)}, u32[]{:S(2)}, u32[]{:S(2)}) collective-permute-start(f32[128,128]{1,0:T(8,128)S(1)} %get-tuple-element.83), channel_id=1, source_target_pairs={{0,4},{4,0},{8,12},{12,8},{16,20},{20,16},{24,28},{28,24},{32,36},... | collective-permute-start | bytes 196616 | tf_op jit(solution)/shard_map/ppermute | solution.py:287
  (1 other events, 0.8 us)

commit v3 on v1

--- a/solution.py
+++ b/solution.py
@@ -17,7 +17,7 @@
 HEAD = 16
 XS = 4
 CORES = 2
-VMEM_LIMIT = 60 * 1024 * 1024
+VMEM_LIMIT = 20 * 1024 * 1024
 COST = pl.CostEstimate(flops=1, bytes_accessed=1, transcendentals=0)
 BF16 = jnp.bfloat16
 F32 = jnp.float32

time: 119 us -> 122 us (1.025)
  Pallas kernels: 43.5 us -> 34.4 us
  waiting for transfers between devices: 19 us -> 24 us
  local copies, waits for them, and re-layouts: 7.92 us -> 11.7 us
  other arithmetic: 3.57 us -> 6.86 us
    pallas_call x3, Pallas kernels: 10.3 us -> 5.11 us  [ends_part(): pl.pallas_call(functools.partial(ends_kernel, count=count), out_shape=jax...]
    ppermute x6, waiting for transfers between devices: 15.4 us -> 20.1 us  [shift_y(): lax.ppermute(value, 'chan', [(n, (n + by) % chans) for n in range(chans)])]
    unnamed x20 -> x18, local copies, waits for them, and re-layouts: 3.28 us -> 6.93 us
    pallas_call x1, Pallas kernels: 15.4 us -> 13.6 us  [response_part(): pl.pallas_call(response_kernel, out_shape=jax.ShapeDtypeStruct((count * t...]
    pallas_call x1, Pallas kernels: 13.7 us -> 12.3 us  [featurize(): pl.pallas_call(featurize_kernel, out_shape=(jax.ShapeDtypeStruct((2, rows...]
  transfers between devices with their start and end apart: 16 -> 16, of which waited for: 6 -> 5; matrix products, arithmetic and copies ran while one was open for 7% -> 8% of each run, Pallas kernels for 20% -> 14%
where the time goes in v3:
time: 122 us
  starting transfers between devices  43.1 us (35%)
  Pallas kernels  34.4 us (28%)
  waiting for transfers between devices  24 us (20%)
  local copies, waits for them, and re-layouts  11.7 us (10%)
  other arithmetic  6.86 us (6%)
  matrix products  1.27 us (1%)
    ppermute x9, starting transfers between devices, permute(): return lax.ppermute(value, 'seq', pairs)  29.8 us
    ppermute x6, waiting for transfers between devices, shift_y(): lax.ppermute(value, 'chan', [(n, (n + by) % chans) for n in range(chans)])  20.1 us
    pallas_call x1, Pallas kernels, response_part(): pl.pallas_call(response_kernel, out_shape=jax.ShapeDtypeStruct((count * t...  13.6 us
    pallas_call x1, Pallas kernels, featurize(): pl.pallas_call(featurize_kernel, out_shape=(jax.ShapeDtypeStruct((2, rows...  12.3 us
    ppermute x6, starting transfers between devices, shift_y(): lax.ppermute(value, 'chan', [(n, (n + by) % chans) for n in range(chans)])  9.33 us
    unnamed x18, local copies, waits for them, and re-layouts  6.93 us
    pallas_call x3, Pallas kernels, ends_part(): pl.pallas_call(functools.partial(ends_kernel, count=count), out_shape=jax...  5.11 us
    ppermute x1, starting transfers between devices, local(): halo = lax.ppermute(raw[:, -LEAD:, :], ('seq', 'chan'), following)  4.02 us
  transfers between devices with their start and end apart: 16, of which 5 were waited for; matrix products, arithmetic and copies ran while one was open for 8% of the time, Pallas kernels for 14%

profile of v3, /device:TPU:1, one launch (start us, length us, event | category | flops | bytes accessed | tf_op | source)
XLA Modules:
  0.0 121.7 jit_solution(9358820747727839211)
XLA Ops:
  0.0 1.8 %slice.12 = bf16[3,8,8192]{2,1,0:T(8,128)(2,1)} slice(bf16[3,128,8192]{2,1,0:T(8,128)(2,1)} %bitcast.144), slice={[0:3], [120:128], [0:8192]} | slice | bytes 786432 | tf_op jit(solution)/shard_map/slice | solution.py:303
  1.8 4.0 %collective-permute-start = (bf16[3,8,8192]{2,1,0:T(8,128)(2,1)}, bf16[3,8,8192]{2,1,0:T(8,128)(2,1)}, u32[]{:S(2)}, u32[]{:S(2)}) collective-permute-start(bf16[3,8,8192]{2,1,0:T(8,128)(2,1)} %slice.12), channel_id=1, source_target_pairs={{0,1},{1,2},{2,3},{3,4},{4,5},{5,6},{6,7},{7,8},{8,9},{9,10},{10,1... | collective-permute-start | bytes 1179656 | tf_op jit(solution)/shard_map/ppermute | solution.py:303
  8.3 1.3 %fusion.23 = f32[128,1344]{0,1:T(8,128)S(1)} fusion(f32[8,128]{1,0:T(8,128)S(1)} %reshape.63, f32[1344,8]{0,1:T(8,128)S(1)} %reshape.65), kind=kOutput, calls=%fused_computation.60 | convolution fusion | flops 16515072 | bytes 735232 | tf_op jit(solution)/shard_map/dot_general | solution.py:307
  9.5 2.8 %copy-done = bf16[128,3,8192]{2,0,1:T(8,128)(2,1)S(1)} copy-done((bf16[128,3,8192]{2,0,1:T(8,128)(2,1)S(1)}, bf16[128,3,8192]{2,0,1:T(8,128)(2,1)}, u32[]{:S(2)}) %copy-start) | copy-done | bytes 6291480
  12.3 12.3 %featurize.1 = (bf16[2,1024,128]{2,1,0:T(8,128)(2,1)S(1)}, bf16[2,1024,128]{2,1,0:T(8,128)(2,1)S(1)}, bf16[2,1024,128]{2,1,0:T(8,128)(2,1)S(1)}, bf16[2,1024,128...) custom-call(s32[8]{0:T(128)S(1)} %stack.64.chunks_ref, ...), custom_call_target="tpu_custom_call" | custom-call | flops 1 | bytes 1 | tf_op jit(solution)/shard_map/featurize/pallas_call | solution.py:81
  24.6 3.4 %featurize_head.1 = (bf16[2,1024,128]{2,1,0:T(8,128)(2,1)S(1)}, bf16[2,1024,128]{2,1,0:T(8,128)(2,1)S(1)}, bf16[2,1024,128]{2,1,0:T(8,128)(2,1)S(1)}, bf16[2,102...) custom-call(s32[8]{0:T(128)S(1)} %stack.64.chunks_ref, ...), custom_call_target="tpu_custom_call", output_to_operand_aliasing={{0}: (4, {}), {1}: (5, {}), {2}: (6, {}), {3}: (7, {}), {4}... | custom-call | flops 1 | bytes 1 | tf_op jit(solution)/shard_map/featurize_head/pallas_call | solution.py:122
  29.6 2.6 %collective-permute-start.1 = (bf16[2,1024,128]{2,1,0:T(8,128)(2,1)}, bf16[2,1024,128]{2,1,0:T(8,128)(2,1)S(1)}, u32[]{:S(2)}, u32[]{:S(2)}) collective-permute-start(bf16[2,1024,128]{2,1,0:T(8,128)(2,1)} %get-tuple-element.60), channel_id=1, source_target_pairs={{0,2},{1,3},{2,0},{3,1},{4,6},{5,7},{6,4},{7,5},{8,10},{9,11},{10,... | collective-permute-start | bytes 1572872 | tf_op jit(solution)/shard_map/ppermute | solution.py:290
  33.1 1.8 %collective-permute-start.3 = (bf16[2,1024,128]{2,1,0:T(8,128)(2,1)}, bf16[2,1024,128]{2,1,0:T(8,128)(2,1)S(1)}, u32[]{:S(2)}, u32[]{:S(2)}) collective-permute-start(bf16[2,1024,128]{2,1,0:T(8,128)(2,1)} %get-tuple-element.62), channel_id=1, source_target_pairs={{0,3},{1,0},{2,1},{3,2},{4,7},{5,4},{6,5},{7,6},{8,11},{9,8},{10,9... | collective-permute-start | bytes 1572872 | tf_op jit(solution)/shard_map/ppermute | solution.py:290
  35.9 1.3 %block_ends.5 = f32[2,128,128]{2,1,0:T(8,128)S(1)} custom-call(bf16[2,1024,128]{2,1,0:T(8,128)(2,1)S(1)} %get-tuple-element.69.refs_0_.rest_3_, f32[2,128,128]{2,1,0:T(8,128)S(1)} %get-tuple-element.86.refs_1_.refs_2_.decay_ref), custom_call_target="tpu_custom_call" | custom-call | flops 1 | bytes 1 | tf_op jit(solution)/shard_map/block_ends/pallas_call | solution.py:189
  37.1 6.0 %collective-permute-done.1.refs_0_.rest_0_ = bf16[2,1024,128]{2,1,0:T(8,128)(2,1)S(1)} collective-permute-done((bf16[2,1024,128]{2,1,0:T(8,128)(2,1)}, bf16[2,1024,128]{2,1,0:T(8,128)(2,1)S(1)}, u32[]{:S(2)}, u32[]{:S(2)}) %collective-permute-start.1) | collective-permute-done | bytes 524320 | tf_op jit(solution)/shard_map/ppermute | solution.py:290
  43.2 1.3 %block_ends.3 = f32[2,128,128]{2,1,0:T(8,128)S(1)} custom-call(bf16[2,1024,128]{2,1,0:T(8,128)(2,1)S(1)} %collective-permute-done.1.refs_0_.rest_0_, f32[2,128,128]{2,1,0:T(8,128)S(1)} %get-tuple-element.86.refs_1_.refs_2_.decay_ref), custom_call_target="tpu_custom_call" | custom-call | flops 1 | bytes 1 | tf_op jit(solution)/shard_map/block_ends/pallas_call | solution.py:189
  44.4 14.0 %collective-permute-done.2.refs_0_.rest_1_ = bf16[2,1024,128]{2,1,0:T(8,128)(2,1)S(1)} collective-permute-done((bf16[2,1024,128]{2,1,0:T(8,128)(2,1)}, bf16[2,1024,128]{2,1,0:T(8,128)(2,1)S(1)}, u32[]{:S(2)}, u32[]{:S(2)}) %collective-permute-start.2) | collective-permute-done | bytes 524320 | tf_op jit(solution)/shard_map/ppermute | solution.py:290
  58.5 2.6 %block_ends.4 = f32[4,128,128]{2,1,0:T(8,128)S(1)} custom-call(bf16[2,1024,128]{2,1,0:T(8,128)(2,1)S(1)} %collective-permute-done.2.refs_0_.rest_1_, bf16[2,1024,128]{2,1,0:T(8,128)(2,1)S(1)} %collective-permute-done.3.refs_1_.rest_2_, f32[2,128,128]{2,1,0:T(8,128)S(1)} %get-tuple-element.86.refs_1_.refs_2_.decay_ref), custom_call_target="tpu_custom_call" | custom-call | flops 1 | bytes 1 | tf_op jit(solution)/shard_map/block_ends/pallas_call | solution.py:189
  66.2 1.4 %collective-permute-start.6 = (f32[128,128]{1,0:T(8,128)S(1)}, f32[128,128]{1,0:T(8,128)S(1)}, u32[]{:S(2)}, u32[]{:S(2)}) collective-permute-start(f32[128,128]{1,0:T(8,128)S(1)} %fusion.17), channel_id=1, source_target_pairs={{0,8},{4,12},{8,16},{12,20},{16,24},{20,28},{24,0},{28,4},{32,40},... | collective-permute-start | bytes 196616 | tf_op jit(solution)/shard_map/ppermute | solution.py:287
  67.7 2.5 %collective-permute-start.7 = (f32[128,128]{1,0:T(8,128)S(1)}, f32[128,128]{1,0:T(8,128)}, u32[]{:S(2)}, u32[]{:S(2)}) collective-permute-start(f32[128,128]{1,0:T(8,128)S(1)} %fusion.17), channel_id=1, source_target_pairs={{0,16},{4,20},{8,24},{12,28},{16,0},{20,4},{24,8},{28,12},{32,48},... | collective-permute-start | bytes 196616 | tf_op jit(solution)/shard_map/ppermute | solution.py:287
  71.3 1.3 %collective-permute-start.12 = (bf16[2,1024,128]{2,1,0:T(8,128)(2,1)}, bf16[2,1024,128]{2,1,0:T(8,128)(2,1)S(1)}, u32[]{:S(2)}, u32[]{:S(2)}) collective-permute-start(bf16[2,1024,128]{2,1,0:T(8,128)(2,1)} %copy-done.1), channel_id=1, source_target_pairs={{0,1},{1,2},{2,3},{3,0},{4,5},{5,6},{6,7},{7,4},{8,9},{9,10},{10,1... | collective-permute-start | bytes 1572872 | tf_op jit(solution)/shard_map/ppermute | solution.py:290
  72.6 2.7 %collective-permute-start.13 = (bf16[2,1024,128]{2,1,0:T(8,128)(2,1)}, bf16[2,1024,128]{2,1,0:T(8,128)(2,1)S(1)}, u32[]{:S(2)}, u32[]{:S(2)}) collective-permute-start(bf16[2,1024,128]{2,1,0:T(8,128)(2,1)} %copy-done.2), channel_id=1, source_target_pairs={{0,3},{1,0},{2,1},{3,2},{4,7},{5,4},{6,5},{7,6},{8,11},{9,8},{10,9... | collective-permute-start | bytes 1572872 | tf_op jit(solution)/shard_map/ppermute | solution.py:290
  76.3 4.9 %collective-permute-start.10 = (f32[128,128]{1,0:T(8,128)S(1)}, f32[128,128]{1,0:T(8,128)S(1)}, u32[]{:S(2)}, u32[]{:S(2)}) collective-permute-start(f32[128,128]{1,0:T(8,128)S(1)} %fusion.14), channel_id=1, source_target_pairs={{0,64},{4,68},{8,72},{12,76},{16,80},{20,84},{24,88},{28,92},{32,9... | collective-permute-start | bytes 196616 | tf_op jit(solution)/shard_map/ppermute | solution.py:287
  81.2 6.6 %collective-permute-start.11 = (f32[128,128]{1,0:T(8,128)S(1)}, f32[128,128]{1,0:T(8,128)S(1)}, u32[]{:S(2)}, u32[]{:S(2)}) collective-permute-start(f32[128,128]{1,0:T(8,128)S(1)} %fusion.14), channel_id=1, source_target_pairs={{0,96},{4,100},{8,104},{12,108},{16,112},{20,116},{24,120},{28,124... | collective-permute-start | bytes 196616 | tf_op jit(solution)/shard_map/ppermute | solution.py:287
  87.8 2.6 %collective-permute-start.9 = (f32[128,128]{1,0:T(8,128)S(1)}, f32[128,128]{1,0:T(8,128)S(1)}, u32[]{:S(2)}, u32[]{:S(2)}) collective-permute-start(f32[128,128]{1,0:T(8,128)S(1)} %fusion.14), channel_id=1, source_target_pairs={{0,32},{4,36},{8,40},{12,44},{16,48},{20,52},{24,56},{28,60},{32,6... | collective-permute-start | bytes 196616 | tf_op jit(solution)/shard_map/ppermute | solution.py:287
  90.4 1.9 %collective-permute-done.9 = f32[128,128]{1,0:T(8,128)S(1)} collective-permute-done((f32[128,128]{1,0:T(8,128)S(1)}, f32[128,128]{1,0:T(8,128)S(1)}, u32[]{:S(2)}, u32[]{:S(2)}) %collective-permute-start.9) | collective-permute-done | bytes 65568 | tf_op jit(solution)/shard_map/ppermute | solution.py:287
  93.8 6.8 %collective-permute-start.14 = (f32[128,128]{1,0:T(8,128)}, f32[128,128]{1,0:T(8,128)}, u32[]{:S(2)}, u32[]{:S(2)}) collective-permute-start(f32[128,128]{1,0:T(8,128)} %get-tuple-element.74), channel_id=1, source_target_pairs={{0,128},{4,132},{8,136},{12,140},{16,144},{20,148},{24,152},{28,15... | collective-permute-start | bytes 196616 | tf_op jit(solution)/shard_map/ppermute | solution.py:287
  102.9 3.2 %collective-permute-start.15 = (f32[128,128]{1,0:T(8,128)S(1)}, f32[128,128]{1,0:T(8,128)S(1)}, u32[]{:S(2)}, u32[]{:S(2)}) collective-permute-start(f32[128,128]{1,0:T(8,128)S(1)} %get-tuple-element.79), channel_id=1, source_target_pairs={{0,4},{4,0},{8,12},{12,8},{16,20},{20,16},{24,28},{28,24},{32,36},... | collective-permute-start | bytes 196616 | tf_op jit(solution)/shard_map/ppermute | solution.py:287
  108.1 13.6 %response.1 = bf16[512,2048]{1,0:T(8,128)(2,1)} custom-call(s32[4]{0:T(128)S(1)} %pad_add_fusion.place_ref, f32[2,128,128]{2,1,0:T(8,128)S(1)} %pad_maximum_fusion.starts_ref, f32[2,128,128]{2,1,0:T(8,128)S(1)} %get-tuple-element.86.refs_1_.refs_2_.decay_ref, f32[2,128,128]{2,1,0:T(8,128)S(1)} %bitcast.149, ...), custom_call_target="tpu_custom_call" | custom-call | flops 1 | bytes 1 | tf_op jit(solution)/shard_map/response/pallas_call | solution.py:250
  (54 shorter events, 18.7 us)
Async XLA Ops:
  1.8 22.8 %collective-permute-start = (bf16[3,8,8192]{2,1,0:T(8,128)(2,1)}, bf16[3,8,8192]{2,1,0:T(8,128)(2,1)}, u32[]{:S(2)}, u32[]{:S(2)}) collective-permute-start(bf16[3,8,8192]{2,1,0:T(8,128)(2,1)} %slice.12), channel_id=1, source_target_pairs={{0,1},{1,2},{2,3},{3,4},{4,5},{5,6},{6,7},{7,8},{8,9},{9,10},{10,1... | collective-permute-start | bytes 1179656 | tf_op jit(solution)/shard_map/ppermute | solution.py:303
  9.5 2.8 %copy-start = (bf16[128,3,8192]{2,0,1:T(8,128)(2,1)S(1)}, bf16[128,3,8192]{2,0,1:T(8,128)(2,1)}, u32[]{:S(2)}) copy-start(bf16[128,3,8192]{2,0,1:T(8,128)(2,1)} %param.4) | copy-start | bytes 18874372
  24.6 10.3 %copy-start.6 = (f32[16,2048]{1,0:T(8,128)S(1)}, f32[16,2048]{1,0:T(8,128)}, u32[]{:S(2)}) copy-start(f32[16,2048]{1,0:T(8,128)} %param.6) | copy-start | bytes 393220
  28.0 0.8 copy-start.1
  28.8 0.8 copy-start.2
  29.6 13.5 %collective-permute-start.1 = (bf16[2,1024,128]{2,1,0:T(8,128)(2,1)}, bf16[2,1024,128]{2,1,0:T(8,128)(2,1)S(1)}, u32[]{:S(2)}, u32[]{:S(2)}) collective-permute-start(bf16[2,1024,128]{2,1,0:T(8,128)(2,1)} %get-tuple-element.60), channel_id=1, source_target_pairs={{0,2},{1,3},{2,0},{3,1},{4,6},{5,7},{6,4},{7,5},{8,10},{9,11},{10,... | collective-permute-start | bytes 1572872 | tf_op jit(solution)/shard_map/ppermute | solution.py:290
  32.3 26.2 %collective-permute-start.2 = (bf16[2,1024,128]{2,1,0:T(8,128)(2,1)}, bf16[2,1024,128]{2,1,0:T(8,128)(2,1)S(1)}, u32[]{:S(2)}, u32[]{:S(2)}) collective-permute-start(bf16[2,1024,128]{2,1,0:T(8,128)(2,1)} %get-tuple-element.61), channel_id=1, source_target_pairs={{0,1},{1,2},{2,3},{3,0},{4,5},{5,6},{6,7},{7,4},{8,9},{9,10},{10,1... | collective-permute-start | bytes 1572872 | tf_op jit(solution)/shard_map/ppermute | solution.py:290
  33.1 25.4 %collective-permute-start.3 = (bf16[2,1024,128]{2,1,0:T(8,128)(2,1)}, bf16[2,1024,128]{2,1,0:T(8,128)(2,1)S(1)}, u32[]{:S(2)}, u32[]{:S(2)}) collective-permute-start(bf16[2,1024,128]{2,1,0:T(8,128)(2,1)} %get-tuple-element.62), channel_id=1, source_target_pairs={{0,3},{1,0},{2,1},{3,2},{4,7},{5,4},{6,5},{7,6},{8,11},{9,8},{10,9... | collective-permute-start | bytes 1572872 | tf_op jit(solution)/shard_map/ppermute | solution.py:290
  35.9 30.4 %collective-permute-start.5 = (bf16[2,1024,128]{2,1,0:T(8,128)(2,1)S(1)}, bf16[2,1024,128]{2,1,0:T(8,128)(2,1)}, u32[]{:S(2)}, u32[]{:S(2)}) collective-permute-start(bf16[2,1024,128]{2,1,0:T(8,128)(2,1)S(1)} %get-tuple-element.70), channel_id=1, source_target_pairs={{0,2},{1,3},{2,0},{3,1},{4,6},{5,7},{6,4},{7,5},{8,10},{9,11},{10,... | collective-permute-start | bytes 1572872 | tf_op jit(solution)/shard_map/ppermute | solution.py:290
  62.2 0.7 copy-start.5
  63.5 1.8 %collective-permute-start.4 = (f32[128,128]{1,0:T(8,128)}, f32[128,128]{1,0:T(8,128)}, u32[]{:S(2)}, u32[]{:S(2)}) collective-permute-start(f32[128,128]{1,0:T(8,128)} %dynamic-slice_bitcast_fusion), channel_id=1, source_target_pairs={{0,4},{4,0},{8,12},{12,8},{16,20},{20,16},{24,28},{28,24},{32,36},... | collective-permute-start | bytes 196616 | tf_op jit(solution)/shard_map/ppermute | solution.py:287
  66.2 9.1 %collective-permute-start.6 = (f32[128,128]{1,0:T(8,128)S(1)}, f32[128,128]{1,0:T(8,128)S(1)}, u32[]{:S(2)}, u32[]{:S(2)}) collective-permute-start(f32[128,128]{1,0:T(8,128)S(1)} %fusion.17), channel_id=1, source_target_pairs={{0,8},{4,12},{8,16},{12,20},{16,24},{20,28},{24,0},{28,4},{32,40},... | collective-permute-start | bytes 196616 | tf_op jit(solution)/shard_map/ppermute | solution.py:287
  67.7 7.6 %collective-permute-start.7 = (f32[128,128]{1,0:T(8,128)S(1)}, f32[128,128]{1,0:T(8,128)}, u32[]{:S(2)}, u32[]{:S(2)}) collective-permute-start(f32[128,128]{1,0:T(8,128)S(1)} %fusion.17), channel_id=1, source_target_pairs={{0,16},{4,20},{8,24},{12,28},{16,0},{20,4},{24,8},{28,12},{32,48},... | collective-permute-start | bytes 196616 | tf_op jit(solution)/shard_map/ppermute | solution.py:287
  70.1 5.2 %collective-permute-start.8 = (f32[128,128]{1,0:T(8,128)S(1)}, f32[128,128]{1,0:T(8,128)}, u32[]{:S(2)}, u32[]{:S(2)}) collective-permute-start(f32[128,128]{1,0:T(8,128)S(1)} %fusion.17), channel_id=1, source_target_pairs={{0,24},{4,28},{8,0},{12,4},{16,8},{20,12},{24,16},{28,20},{32,56},... | collective-permute-start | bytes 196616 | tf_op jit(solution)/shard_map/ppermute | solution.py:287
  71.3 21.7 %collective-permute-start.12 = (bf16[2,1024,128]{2,1,0:T(8,128)(2,1)}, bf16[2,1024,128]{2,1,0:T(8,128)(2,1)S(1)}, u32[]{:S(2)}, u32[]{:S(2)}) collective-permute-start(bf16[2,1024,128]{2,1,0:T(8,128)(2,1)} %copy-done.1), channel_id=1, source_target_pairs={{0,1},{1,2},{2,3},{3,0},{4,5},{5,6},{6,7},{7,4},{8,9},{9,10},{10,1... | collective-permute-start | bytes 1572872 | tf_op jit(solution)/shard_map/ppermute | solution.py:290
  72.6 20.4 %collective-permute-start.13 = (bf16[2,1024,128]{2,1,0:T(8,128)(2,1)}, bf16[2,1024,128]{2,1,0:T(8,128)(2,1)S(1)}, u32[]{:S(2)}, u32[]{:S(2)}) collective-permute-start(bf16[2,1024,128]{2,1,0:T(8,128)(2,1)} %copy-done.2), channel_id=1, source_target_pairs={{0,3},{1,0},{2,1},{3,2},{4,7},{5,4},{6,5},{7,6},{8,11},{9,8},{10,9... | collective-permute-start | bytes 1572872 | tf_op jit(solution)/shard_map/ppermute | solution.py:290
  75.3 18.5 %copy-start.7 = (f32[128,128]{1,0:T(8,128)}, f32[128,128]{1,0:T(8,128)S(1)}, u32[]{:S(2)}) copy-start(f32[128,128]{1,0:T(8,128)S(1)} %collective-permute-done.6) | copy-start | bytes 196612
  76.3 14.1 %collective-permute-start.10 = (f32[128,128]{1,0:T(8,128)S(1)}, f32[128,128]{1,0:T(8,128)S(1)}, u32[]{:S(2)}, u32[]{:S(2)}) collective-permute-start(f32[128,128]{1,0:T(8,128)S(1)} %fusion.14), channel_id=1, source_target_pairs={{0,64},{4,68},{8,72},{12,76},{16,80},{20,84},{24,88},{28,92},{32,9... | collective-permute-start | bytes 196616 | tf_op jit(solution)/shard_map/ppermute | solution.py:287
  81.2 9.2 %collective-permute-start.11 = (f32[128,128]{1,0:T(8,128)S(1)}, f32[128,128]{1,0:T(8,128)S(1)}, u32[]{:S(2)}, u32[]{:S(2)}) collective-permute-start(f32[128,128]{1,0:T(8,128)S(1)} %fusion.14), channel_id=1, source_target_pairs={{0,96},{4,100},{8,104},{12,108},{16,112},{20,116},{24,120},{28,124... | collective-permute-start | bytes 196616 | tf_op jit(solution)/shard_map/ppermute | solution.py:287
  87.8 4.5 %collective-permute-start.9 = (f32[128,128]{1,0:T(8,128)S(1)}, f32[128,128]{1,0:T(8,128)S(1)}, u32[]{:S(2)}, u32[]{:S(2)}) collective-permute-start(f32[128,128]{1,0:T(8,128)S(1)} %fusion.14), channel_id=1, source_target_pairs={{0,32},{4,36},{8,40},{12,44},{16,48},{20,52},{24,56},{28,60},{32,6... | collective-permute-start | bytes 196616 | tf_op jit(solution)/shard_map/ppermute | solution.py:287
  93.0 0.8 copy-start.3
  93.8 7.9 %collective-permute-start.14 = (f32[128,128]{1,0:T(8,128)}, f32[128,128]{1,0:T(8,128)}, u32[]{:S(2)}, u32[]{:S(2)}) collective-permute-start(f32[128,128]{1,0:T(8,128)} %get-tuple-element.74), channel_id=1, source_target_pairs={{0,128},{4,132},{8,136},{12,140},{16,144},{20,148},{24,152},{28,15... | collective-permute-start | bytes 196616 | tf_op jit(solution)/shard_map/ppermute | solution.py:287
  102.9 4.1 %collective-permute-start.15 = (f32[128,128]{1,0:T(8,128)S(1)}, f32[128,128]{1,0:T(8,128)S(1)}, u32[]{:S(2)}, u32[]{:S(2)}) collective-permute-start(f32[128,128]{1,0:T(8,128)S(1)} %get-tuple-element.79), channel_id=1, source_target_pairs={{0,4},{4,0},{8,12},{12,8},{16,20},{20,16},{24,28},{28,24},{32,36},... | collective-permute-start | bytes 196616 | tf_op jit(solution)/shard_map/ppermute | solution.py:287
  107.0 1.0 copy-start.4

commit v4 on v1

--- a/solution.py
+++ b/solution.py
@@ -18,6 +18,7 @@
 XS = 4
 CORES = 2
 VMEM_LIMIT = 60 * 1024 * 1024
+VMEM_SMALL = 20 * 1024 * 1024
 COST = pl.CostEstimate(flops=1, bytes_accessed=1, transcendentals=0)
 BF16 = jnp.bfloat16
 F32 = jnp.float32
@@ -192,7 +193,7 @@
         grid=(2 * count,),
         in_specs=[turn(n) for n in range(count)] + [pl.BlockSpec(state, lambda i: (i % 2, 0, 0))],
         out_specs=pl.BlockSpec(state, lambda i: (i, 0, 0)),
-        compiler_params=pltpu.CompilerParams(vmem_limit_bytes=VMEM_LIMIT),
+        compiler_params=pltpu.CompilerParams(vmem_limit_bytes=VMEM_SMALL),
         cost_estimate=COST,
         name="block_ends",
     )(*gated, decay)
@@ -260,7 +261,7 @@
                 pltpu.VMEM((rows, LANES), F32),
             ],
         ),
-        compiler_params=pltpu.CompilerParams(vmem_limit_bytes=VMEM_LIMIT),
+        compiler_params=pltpu.CompilerParams(vmem_limit_bytes=VMEM_SMALL),
         cost_estimate=COST,
         name="response",
     )(places, starts, decay, gain, *gated, *queries)

time: 119 us -> 122 us (1.025)
  Pallas kernels: 43.5 us -> 35.4 us
  waiting for transfers between devices: 19 us -> 23.1 us
  other arithmetic: 3.57 us -> 6.86 us
  local copies, waits for them, and re-layouts: 7.92 us -> 10.8 us
    pallas_call x3, Pallas kernels: 10.3 us -> 5.11 us  [ends_part(): pl.pallas_call(functools.partial(ends_kernel, count=count), out_shape=jax...]
    ppermute x6, waiting for transfers between devices: 15.4 us -> 19.1 us  [shift_y(): lax.ppermute(value, 'chan', [(n, (n + by) % chans) for n in range(chans)])]
    unnamed x20 -> x24, local copies, waits for them, and re-layouts: 3.28 us -> 6.18 us
    pallas_call x1, Pallas kernels: 15.4 us -> 12.6 us  [response_part(): pl.pallas_call(response_kernel, out_shape=jax.ShapeDtypeStruct((count * t...]
  transfers between devices with their start and end apart: 16 -> 16, of which waited for: 6 -> 6; matrix products, arithmetic and copies ran while one was open for 7% -> 9% of each run, Pallas kernels for 20% -> 15%
where the time goes in v4:
time: 122 us
  starting transfers between devices  43 us (35%)
  Pallas kernels  35.4 us (29%)
  waiting for transfers between devices  23.1 us (19%)
  local copies, waits for them, and re-layouts  10.8 us (9%)
  other arithmetic  6.86 us (6%)
  matrix products  2.11 us (2%)
    ppermute x9, starting transfers between devices, permute(): return lax.ppermute(value, 'seq', pairs)  29.6 us
    ppermute x6, waiting for transfers between devices, shift_y(): lax.ppermute(value, 'chan', [(n, (n + by) % chans) for n in range(chans)])  19.1 us
    pallas_call x1, Pallas kernels, featurize(): pl.pallas_call(featurize_kernel, out_shape=(jax.ShapeDtypeStruct((2, rows...  13.6 us
    pallas_call x1, Pallas kernels, response_part(): pl.pallas_call(response_kernel, out_shape=jax.ShapeDtypeStruct((count * t...  12.6 us
    ppermute x6, starting transfers between devices, shift_y(): lax.ppermute(value, 'chan', [(n, (n + by) % chans) for n in range(chans)])  9.43 us
    unnamed x24, local copies, waits for them, and re-layouts  6.18 us
    pallas_call x3, Pallas kernels, ends_part(): pl.pallas_call(functools.partial(ends_kernel, count=count), out_shape=jax...  5.11 us
    pallas_call x1, Pallas kernels, featurize_head(): pl.pallas_call(head_kernel, out_shape=tuple((jax.ShapeDtypeStruct(v.shape...  4.13 us
  transfers between devices with their start and end apart: 16, of which 6 were waited for; matrix products, arithmetic and copies ran while one was open for 9% of the time, Pallas kernels for 15%

profile of v4, /device:TPU:1, one launch (start us, length us, event | category | flops | bytes accessed | tf_op | source)
XLA Modules:
  0.0 121.6 jit_solution(12350727739901917119)
XLA Ops:
  1.0 4.0 %collective-permute-start = (bf16[3,8,8192]{2,1,0:T(8,128)(2,1)S(1)}, bf16[3,8,8192]{2,1,0:T(8,128)(2,1)S(1)}, u32[]{:S(2)}, u32[]{:S(2)}) collective-permute-start(bf16[3,8,8192]{2,1,0:T(8,128)(2,1)S(1)} %slice.12), channel_id=1, source_target_pairs={{0,1},{1,2},{2,3},{3,4},{4,5},{5,6},{6,7},{7,8},{8,9},{9,10},{10,1... | collective-permute-start | bytes 1179656 | tf_op jit(solution)/shard_map/ppermute | solution.py:304
  5.1 1.2 reshape.64
  8.1 2.1 %fusion.23 = f32[128,1344]{0,1:T(8,128)} fusion(f32[8,128]{1,0:T(8,128)S(1)} %reshape.63, f32[1344,8]{0,1:T(8,128)S(1)} %reshape.65), kind=kOutput, calls=%fused_computation.60 | convolution fusion | flops 16515072 | bytes 735232 | tf_op jit(solution)/shard_map/dot_general | solution.py:308
  10.2 13.6 %featurize.1 = (bf16[2,1024,128]{2,1,0:T(8,128)(2,1)}, bf16[2,1024,128]{2,1,0:T(8,128)(2,1)}, bf16[2,1024,128]{2,1,0:T(8,128)(2,1)}, bf16[2,1024,128]{2,1,0:T(8,...) custom-call(s32[8]{0:T(128)} %stack.64.chunks_ref, ...), custom_call_target="tpu_custom_call" | custom-call | flops 1 | bytes 1 | tf_op jit(solution)/shard_map/featurize/pallas_call | solution.py:82
  24.6 4.1 %featurize_head.1 = (bf16[2,1024,128]{2,1,0:T(8,128)(2,1)}, bf16[2,1024,128]{2,1,0:T(8,128)(2,1)}, bf16[2,1024,128]{2,1,0:T(8,128)(2,1)}, bf16[2,1024,128]{2,1,0...) custom-call(s32[8]{0:T(128)} %stack.64.chunks_ref, ...), custom_call_target="tpu_custom_call", output_to_operand_aliasing={{0}: (4, {}), {1}: (5, {}), {2}: (6, {}), {3}: (7, {}), {4}... | custom-call | flops 1 | bytes 1 | tf_op jit(solution)/shard_map/featurize_head/pallas_call | solution.py:123
  28.7 2.7 %collective-permute-start.1 = (bf16[2,1024,128]{2,1,0:T(8,128)(2,1)}, bf16[2,1024,128]{2,1,0:T(8,128)(2,1)S(1)}, u32[]{:S(2)}, u32[]{:S(2)}) collective-permute-start(bf16[2,1024,128]{2,1,0:T(8,128)(2,1)} %get-tuple-element.60), channel_id=1, source_target_pairs={{0,2},{1,3},{2,0},{3,1},{4,6},{5,7},{6,4},{7,5},{8,10},{9,11},{10,... | collective-permute-start | bytes 1572872 | tf_op jit(solution)/shard_map/ppermute | solution.py:291
  32.3 1.8 %collective-permute-start.3 = (bf16[2,1024,128]{2,1,0:T(8,128)(2,1)}, bf16[2,1024,128]{2,1,0:T(8,128)(2,1)S(1)}, u32[]{:S(2)}, u32[]{:S(2)}) collective-permute-start(bf16[2,1024,128]{2,1,0:T(8,128)(2,1)} %get-tuple-element.62), channel_id=1, source_target_pairs={{0,3},{1,0},{2,1},{3,2},{4,7},{5,4},{6,5},{7,6},{8,11},{9,8},{10,9... | collective-permute-start | bytes 1572872 | tf_op jit(solution)/shard_map/ppermute | solution.py:291
  36.1 1.3 %block_ends.5 = f32[2,128,128]{2,1,0:T(8,128)S(1)} custom-call(bf16[2,1024,128]{2,1,0:T(8,128)(2,1)S(1)} %copy-done, f32[2,128,128]{2,1,0:T(8,128)S(1)} %get-tuple-element.86.refs_1_.refs_2_.decay_ref), custom_call_target="tpu_custom_call" | custom-call | flops 1 | bytes 1 | tf_op jit(solution)/shard_map/block_ends/pallas_call | solution.py:190
  37.3 5.7 %collective-permute-done.1.refs_0_.rest_0_ = bf16[2,1024,128]{2,1,0:T(8,128)(2,1)S(1)} collective-permute-done((bf16[2,1024,128]{2,1,0:T(8,128)(2,1)}, bf16[2,1024,128]{2,1,0:T(8,128)(2,1)S(1)}, u32[]{:S(2)}, u32[]{:S(2)}) %collective-permute-start.1) | collective-permute-done | bytes 524320 | tf_op jit(solution)/shard_map/ppermute | solution.py:291
  43.0 1.3 %block_ends.3 = f32[2,128,128]{2,1,0:T(8,128)S(1)} custom-call(bf16[2,1024,128]{2,1,0:T(8,128)(2,1)S(1)} %collective-permute-done.1.refs_0_.rest_0_, f32[2,128,128]{2,1,0:T(8,128)S(1)} %get-tuple-element.86.refs_1_.refs_2_.decay_ref), custom_call_target="tpu_custom_call" | custom-call | flops 1 | bytes 1 | tf_op jit(solution)/shard_map/block_ends/pallas_call | solution.py:190
  44.3 12.7 %collective-permute-done.2.refs_0_.rest_1_ = bf16[2,1024,128]{2,1,0:T(8,128)(2,1)S(1)} collective-permute-done((bf16[2,1024,128]{2,1,0:T(8,128)(2,1)}, bf16[2,1024,128]{2,1,0:T(8,128)(2,1)S(1)}, u32[]{:S(2)}, u32[]{:S(2)}) %collective-permute-start.2) | collective-permute-done | bytes 524320 | tf_op jit(solution)/shard_map/ppermute | solution.py:291
  57.0 2.6 %block_ends.4 = f32[4,128,128]{2,1,0:T(8,128)S(1)} custom-call(bf16[2,1024,128]{2,1,0:T(8,128)(2,1)S(1)} %collective-permute-done.2.refs_0_.rest_1_, bf16[2,1024,128]{2,1,0:T(8,128)(2,1)S(1)} %collective-permute-done.3.refs_1_.rest_2_, f32[2,128,128]{2,1,0:T(8,128)S(1)} %get-tuple-element.86.refs_1_.refs_2_.decay_ref), custom_call_target="tpu_custom_call" | custom-call | flops 1 | bytes 1 | tf_op jit(solution)/shard_map/block_ends/pallas_call | solution.py:190
  62.6 1.2 %collective-permute-done.4 = f32[128,128]{1,0:T(8,128)} collective-permute-done((f32[128,128]{1,0:T(8,128)}, f32[128,128]{1,0:T(8,128)}, u32[]{:S(2)}, u32[]{:S(2)}) %collective-permute-start.4) | collective-permute-done | bytes 65568 | tf_op jit(solution)/shard_map/ppermute | solution.py:288
  65.5 1.2 %collective-permute-start.6 = (f32[128,128]{1,0:T(8,128)S(1)}, f32[128,128]{1,0:T(8,128)S(1)}, u32[]{:S(2)}, u32[]{:S(2)}) collective-permute-start(f32[128,128]{1,0:T(8,128)S(1)} %fusion.17), channel_id=1, source_target_pairs={{0,8},{4,12},{8,16},{12,20},{16,24},{20,28},{24,0},{28,4},{32,40},... | collective-permute-start | bytes 196616 | tf_op jit(solution)/shard_map/ppermute | solution.py:288
  66.7 2.5 %collective-permute-start.7 = (f32[128,128]{1,0:T(8,128)S(1)}, f32[128,128]{1,0:T(8,128)}, u32[]{:S(2)}, u32[]{:S(2)}) collective-permute-start(f32[128,128]{1,0:T(8,128)S(1)} %fusion.17), channel_id=1, source_target_pairs={{0,16},{4,20},{8,24},{12,28},{16,0},{20,4},{24,8},{28,12},{32,48},... | collective-permute-start | bytes 196616 | tf_op jit(solution)/shard_map/ppermute | solution.py:288
  70.3 1.3 %collective-permute-start.12 = (bf16[2,1024,128]{2,1,0:T(8,128)(2,1)}, bf16[2,1024,128]{2,1,0:T(8,128)(2,1)S(1)}, u32[]{:S(2)}, u32[]{:S(2)}) collective-permute-start(bf16[2,1024,128]{2,1,0:T(8,128)(2,1)} %get-tuple-element.72), channel_id=1, source_target_pairs={{0,1},{1,2},{2,3},{3,0},{4,5},{5,6},{6,7},{7,4},{8,9},{9,10},{10,1... | collective-permute-start | bytes 1572872 | tf_op jit(solution)/shard_map/ppermute | solution.py:291
  71.7 2.7 %collective-permute-start.13 = (bf16[2,1024,128]{2,1,0:T(8,128)(2,1)}, bf16[2,1024,128]{2,1,0:T(8,128)(2,1)S(1)}, u32[]{:S(2)}, u32[]{:S(2)}) collective-permute-start(bf16[2,1024,128]{2,1,0:T(8,128)(2,1)} %get-tuple-element.73), channel_id=1, source_target_pairs={{0,3},{1,0},{2,1},{3,2},{4,7},{5,4},{6,5},{7,6},{8,11},{9,8},{10,9... | collective-permute-start | bytes 1572872 | tf_op jit(solution)/shard_map/ppermute | solution.py:291
  75.4 4.9 %collective-permute-start.10 = (f32[128,128]{1,0:T(8,128)S(1)}, f32[128,128]{1,0:T(8,128)S(1)}, u32[]{:S(2)}, u32[]{:S(2)}) collective-permute-start(f32[128,128]{1,0:T(8,128)S(1)} %fusion.14), channel_id=1, source_target_pairs={{0,64},{4,68},{8,72},{12,76},{16,80},{20,84},{24,88},{28,92},{32,9... | collective-permute-start | bytes 196616 | tf_op jit(solution)/shard_map/ppermute | solution.py:288
  80.3 6.6 %collective-permute-start.11 = (f32[128,128]{1,0:T(8,128)S(1)}, f32[128,128]{1,0:T(8,128)S(1)}, u32[]{:S(2)}, u32[]{:S(2)}) collective-permute-start(f32[128,128]{1,0:T(8,128)S(1)} %fusion.14), channel_id=1, source_target_pairs={{0,96},{4,100},{8,104},{12,108},{16,112},{20,116},{24,120},{28,124... | collective-permute-start | bytes 196616 | tf_op jit(solution)/shard_map/ppermute | solution.py:288
  86.8 2.6 %collective-permute-start.9 = (f32[128,128]{1,0:T(8,128)S(1)}, f32[128,128]{1,0:T(8,128)S(1)}, u32[]{:S(2)}, u32[]{:S(2)}) collective-permute-start(f32[128,128]{1,0:T(8,128)S(1)} %fusion.14), channel_id=1, source_target_pairs={{0,32},{4,36},{8,40},{12,44},{16,48},{20,52},{24,56},{28,60},{32,6... | collective-permute-start | bytes 196616 | tf_op jit(solution)/shard_map/ppermute | solution.py:288
  89.5 1.9 %collective-permute-done.9 = f32[128,128]{1,0:T(8,128)S(1)} collective-permute-done((f32[128,128]{1,0:T(8,128)S(1)}, f32[128,128]{1,0:T(8,128)S(1)}, u32[]{:S(2)}, u32[]{:S(2)}) %collective-permute-start.9) | collective-permute-done | bytes 65568 | tf_op jit(solution)/shard_map/ppermute | solution.py:288
  93.7 6.8 %collective-permute-start.14 = (f32[128,128]{1,0:T(8,128)}, f32[128,128]{1,0:T(8,128)}, u32[]{:S(2)}, u32[]{:S(2)}) collective-permute-start(f32[128,128]{1,0:T(8,128)} %get-tuple-element.74), channel_id=1, source_target_pairs={{0,128},{4,132},{8,136},{12,140},{16,144},{20,148},{24,152},{28,15... | collective-permute-start | bytes 196616 | tf_op jit(solution)/shard_map/ppermute | solution.py:288
  102.8 3.2 %collective-permute-start.15 = (f32[128,128]{1,0:T(8,128)S(1)}, f32[128,128]{1,0:T(8,128)S(1)}, u32[]{:S(2)}, u32[]{:S(2)}) collective-permute-start(f32[128,128]{1,0:T(8,128)S(1)} %get-tuple-element.79), channel_id=1, source_target_pairs={{0,4},{4,0},{8,12},{12,8},{16,20},{20,16},{24,28},{28,24},{32,36},... | collective-permute-start | bytes 196616 | tf_op jit(solution)/shard_map/ppermute | solution.py:288
  109.0 12.6 %response.1 = bf16[512,2048]{1,0:T(8,128)(2,1)} custom-call(s32[4]{0:T(128)S(1)} %pad_add_fusion.place_ref, f32[2,128,128]{2,1,0:T(8,128)S(1)} %pad_maximum_fusion.starts_ref, f32[2,128,128]{2,1,0:T(8,128)S(1)} %get-tuple-element.86.refs_1_.refs_2_.decay_ref, f32[2,128,128]{2,1,0:T(8,128)S(1)} %bitcast.144, ...), custom_call_target="tpu_custom_call" | custom-call | flops 1 | bytes 1 | tf_op jit(solution)/shard_map/response/pallas_call | solution.py:251
  (60 shorter events, 20.7 us)
Async XLA Ops:
  1.0 22.8 %collective-permute-start = (bf16[3,8,8192]{2,1,0:T(8,128)(2,1)S(1)}, bf16[3,8,8192]{2,1,0:T(8,128)(2,1)S(1)}, u32[]{:S(2)}, u32[]{:S(2)}) collective-permute-start(bf16[3,8,8192]{2,1,0:T(8,128)(2,1)S(1)} %slice.12), channel_id=1, source_target_pairs={{0,1},{1,2},{2,3},{3,4},{4,5},{5,6},{6,7},{7,8},{8,9},{9,10},{10,1... | collective-permute-start | bytes 1179656 | tf_op jit(solution)/shard_map/ppermute | solution.py:304
  23.8 10.3 %copy-start.8 = (f32[16,2048]{1,0:T(8,128)S(1)}, f32[16,2048]{1,0:T(8,128)}, u32[]{:S(2)}) copy-start(f32[16,2048]{1,0:T(8,128)} %param.6) | copy-start | bytes 393220
  28.7 78.2 %copy-start.1 = (bf16[2,1024,128]{2,1,0:T(8,128)(2,1)S(1)}, bf16[2,1024,128]{2,1,0:T(8,128)(2,1)}, u32[]{:S(2)}) copy-start(bf16[2,1024,128]{2,1,0:T(8,128)(2,1)} %get-tuple-element.69.refs_0_.rest_3_) | copy-start | bytes 1572868
  28.7 78.2 %copy-start.2 = (bf16[2,1024,128]{2,1,0:T(8,128)(2,1)S(1)}, bf16[2,1024,128]{2,1,0:T(8,128)(2,1)}, u32[]{:S(2)}) copy-start(bf16[2,1024,128]{2,1,0:T(8,128)(2,1)} %get-tuple-element.78.rest_7_) | copy-start | bytes 1572868
  28.7 14.3 %collective-permute-start.1 = (bf16[2,1024,128]{2,1,0:T(8,128)(2,1)}, bf16[2,1024,128]{2,1,0:T(8,128)(2,1)S(1)}, u32[]{:S(2)}, u32[]{:S(2)}) collective-permute-start(bf16[2,1024,128]{2,1,0:T(8,128)(2,1)} %get-tuple-element.60), channel_id=1, source_target_pairs={{0,2},{1,3},{2,0},{3,1},{4,6},{5,7},{6,4},{7,5},{8,10},{9,11},{10,... | collective-permute-start | bytes 1572872 | tf_op jit(solution)/shard_map/ppermute | solution.py:291
  31.4 25.5 %collective-permute-start.2 = (bf16[2,1024,128]{2,1,0:T(8,128)(2,1)}, bf16[2,1024,128]{2,1,0:T(8,128)(2,1)S(1)}, u32[]{:S(2)}, u32[]{:S(2)}) collective-permute-start(bf16[2,1024,128]{2,1,0:T(8,128)(2,1)} %get-tuple-element.61), channel_id=1, source_target_pairs={{0,1},{1,2},{2,3},{3,0},{4,5},{5,6},{6,7},{7,4},{8,9},{9,10},{10,1... | collective-permute-start | bytes 1572872 | tf_op jit(solution)/shard_map/ppermute | solution.py:291
  32.3 24.7 %collective-permute-start.3 = (bf16[2,1024,128]{2,1,0:T(8,128)(2,1)}, bf16[2,1024,128]{2,1,0:T(8,128)(2,1)S(1)}, u32[]{:S(2)}, u32[]{:S(2)}) collective-permute-start(bf16[2,1024,128]{2,1,0:T(8,128)(2,1)} %get-tuple-element.62), channel_id=1, source_target_pairs={{0,3},{1,0},{2,1},{3,2},{4,7},{5,4},{6,5},{7,6},{8,11},{9,8},{10,9... | collective-permute-start | bytes 1572872 | tf_op jit(solution)/shard_map/ppermute | solution.py:291
  35.0 30.5 %collective-permute-start.5 = (bf16[2,1024,128]{2,1,0:T(8,128)(2,1)}, bf16[2,1024,128]{2,1,0:T(8,128)(2,1)S(1)}, u32[]{:S(2)}, u32[]{:S(2)}) collective-permute-start(bf16[2,1024,128]{2,1,0:T(8,128)(2,1)} %get-tuple-element.70), channel_id=1, source_target_pairs={{0,2},{1,3},{2,0},{3,1},{4,6},{5,7},{6,4},{7,5},{8,10},{9,11},{10,... | collective-permute-start | bytes 1572872 | tf_op jit(solution)/shard_map/ppermute | solution.py:291
  35.0 1.0 copy-start
  62.0 1.8 %collective-permute-start.4 = (f32[128,128]{1,0:T(8,128)}, f32[128,128]{1,0:T(8,128)}, u32[]{:S(2)}, u32[]{:S(2)}) collective-permute-start(f32[128,128]{1,0:T(8,128)} %dynamic-slice_bitcast_fusion), channel_id=1, source_target_pairs={{0,4},{4,0},{8,12},{12,8},{16,20},{20,16},{24,28},{28,24},{32,36},... | collective-permute-start | bytes 196616 | tf_op jit(solution)/shard_map/ppermute | solution.py:288
  65.5 8.9 %collective-permute-start.6 = (f32[128,128]{1,0:T(8,128)S(1)}, f32[128,128]{1,0:T(8,128)S(1)}, u32[]{:S(2)}, u32[]{:S(2)}) collective-permute-start(f32[128,128]{1,0:T(8,128)S(1)} %fusion.17), channel_id=1, source_target_pairs={{0,8},{4,12},{8,16},{12,20},{16,24},{20,28},{24,0},{28,4},{32,40},... | collective-permute-start | bytes 196616 | tf_op jit(solution)/shard_map/ppermute | solution.py:288
  66.7 7.7 %collective-permute-start.7 = (f32[128,128]{1,0:T(8,128)S(1)}, f32[128,128]{1,0:T(8,128)}, u32[]{:S(2)}, u32[]{:S(2)}) collective-permute-start(f32[128,128]{1,0:T(8,128)S(1)} %fusion.17), channel_id=1, source_target_pairs={{0,16},{4,20},{8,24},{12,28},{16,0},{20,4},{24,8},{28,12},{32,48},... | collective-permute-start | bytes 196616 | tf_op jit(solution)/shard_map/ppermute | solution.py:288
  69.2 5.2 %collective-permute-start.8 = (f32[128,128]{1,0:T(8,128)S(1)}, f32[128,128]{1,0:T(8,128)}, u32[]{:S(2)}, u32[]{:S(2)}) collective-permute-start(f32[128,128]{1,0:T(8,128)S(1)} %fusion.17), channel_id=1, source_target_pairs={{0,24},{4,28},{8,0},{12,4},{16,8},{20,12},{24,16},{28,20},{32,56},... | collective-permute-start | bytes 196616 | tf_op jit(solution)/shard_map/ppermute | solution.py:288
  70.3 21.7 %collective-permute-start.12 = (bf16[2,1024,128]{2,1,0:T(8,128)(2,1)}, bf16[2,1024,128]{2,1,0:T(8,128)(2,1)S(1)}, u32[]{:S(2)}, u32[]{:S(2)}) collective-permute-start(bf16[2,1024,128]{2,1,0:T(8,128)(2,1)} %get-tuple-element.72), channel_id=1, source_target_pairs={{0,1},{1,2},{2,3},{3,0},{4,5},{5,6},{6,7},{7,4},{8,9},{9,10},{10,1... | collective-permute-start | bytes 1572872 | tf_op jit(solution)/shard_map/ppermute | solution.py:291
  71.7 21.2 %collective-permute-start.13 = (bf16[2,1024,128]{2,1,0:T(8,128)(2,1)}, bf16[2,1024,128]{2,1,0:T(8,128)(2,1)S(1)}, u32[]{:S(2)}, u32[]{:S(2)}) collective-permute-start(bf16[2,1024,128]{2,1,0:T(8,128)(2,1)} %get-tuple-element.73), channel_id=1, source_target_pairs={{0,3},{1,0},{2,1},{3,2},{4,7},{5,4},{6,5},{7,6},{8,11},{9,8},{10,9... | collective-permute-start | bytes 1572872 | tf_op jit(solution)/shard_map/ppermute | solution.py:291
  74.4 19.3 %copy-start.10 = (f32[128,128]{1,0:T(8,128)}, f32[128,128]{1,0:T(8,128)S(1)}, u32[]{:S(2)}) copy-start(f32[128,128]{1,0:T(8,128)S(1)} %collective-permute-done.6) | copy-start | bytes 196612
  75.4 14.1 %collective-permute-start.10 = (f32[128,128]{1,0:T(8,128)S(1)}, f32[128,128]{1,0:T(8,128)S(1)}, u32[]{:S(2)}, u32[]{:S(2)}) collective-permute-start(f32[128,128]{1,0:T(8,128)S(1)} %fusion.14), channel_id=1, source_target_pairs={{0,64},{4,68},{8,72},{12,76},{16,80},{20,84},{24,88},{28,92},{32,9... | collective-permute-start | bytes 196616 | tf_op jit(solution)/shard_map/ppermute | solution.py:288
  80.3 9.2 %collective-permute-start.11 = (f32[128,128]{1,0:T(8,128)S(1)}, f32[128,128]{1,0:T(8,128)S(1)}, u32[]{:S(2)}, u32[]{:S(2)}) collective-permute-start(f32[128,128]{1,0:T(8,128)S(1)} %fusion.14), channel_id=1, source_target_pairs={{0,96},{4,100},{8,104},{12,108},{16,112},{20,116},{24,120},{28,124... | collective-permute-start | bytes 196616 | tf_op jit(solution)/shard_map/ppermute | solution.py:288
  86.8 4.5 %collective-permute-start.9 = (f32[128,128]{1,0:T(8,128)S(1)}, f32[128,128]{1,0:T(8,128)S(1)}, u32[]{:S(2)}, u32[]{:S(2)}) collective-permute-start(f32[128,128]{1,0:T(8,128)S(1)} %fusion.14), channel_id=1, source_target_pairs={{0,32},{4,36},{8,40},{12,44},{16,48},{20,52},{24,56},{28,60},{32,6... | collective-permute-start | bytes 196616 | tf_op jit(solution)/shard_map/ppermute | solution.py:288
  92.9 0.8 copy-start.5
  93.7 7.9 %collective-permute-start.14 = (f32[128,128]{1,0:T(8,128)}, f32[128,128]{1,0:T(8,128)}, u32[]{:S(2)}, u32[]{:S(2)}) collective-permute-start(f32[128,128]{1,0:T(8,128)} %get-tuple-element.74), channel_id=1, source_target_pairs={{0,128},{4,132},{8,136},{12,140},{16,144},{20,148},{24,152},{28,15... | collective-permute-start | bytes 196616 | tf_op jit(solution)/shard_map/ppermute | solution.py:288
  102.8 4.1 %collective-permute-start.15 = (f32[128,128]{1,0:T(8,128)S(1)}, f32[128,128]{1,0:T(8,128)S(1)}, u32[]{:S(2)}, u32[]{:S(2)}) collective-permute-start(f32[128,128]{1,0:T(8,128)S(1)} %get-tuple-element.79), channel_id=1, source_target_pairs={{0,4},{4,0},{8,12},{12,8},{16,20},{20,16},{24,28},{28,24},{32,36},... | collective-permute-start | bytes 196616 | tf_op jit(solution)/shard_map/ppermute | solution.py:288
  107.0 1.0 copy-start.4
  108.0 1.0 copy-start.6
  (3 other events, 2.2 us)
